TPU v7x, 512 devices: a whole 4x8x8 slice. The times are simulated.
512 devices in a mesh: seq: 16 (over y, z_hi), mp: 8 (over z_lo, core), leaf: 4 (over x).
Axes of the slice: x: 4, y: 8, z: 8 (z_hi: 2, z_lo: 4; z = z_hi * 4 + z_lo), core: 2. Of those that a mesh axis runs over, the one named last changes fastest.
Arguments:
- queries: bfloat16 [16384, 8192], P(('leaf', 'seq'), 'mp'), parts along dimension 0
- keys: bfloat16 [16384, 1024], P(('leaf', 'seq'), 'mp'), parts along dimension 0
- values: bfloat16 [16384, 1024], P(('leaf', 'seq'), 'mp'), parts along dimension 0, may hold values from -5 to 5
- tree_mask: int32 [64, 16], P('leaf'), parts along dimension 0, may hold values from 0 to 1, as said below
- step_lengths: int32 [64], P('leaf'), parts along dimension 0, may hold values from 2 to 256, as said below
- probe: bfloat16 [8192], P('mp'), may hold values from -0.5 to 0.5
Outputs:
- attended: bfloat16 [16384, 8192], P(('leaf', 'seq'), 'mp'), parts along dimension 0
- step_score: float32 [64], P(('leaf', 'seq')), parts along dimension 0
There are 4 independent parts, one for each index of `leaf`. A program takes and returns all parts, laid end to end along the dimension named above; an argument that names none is the same for every part. Nothing has to cross between parts.
Inputs may be any that keep to these rules, and one draw needn't show every extreme that they name: Block 0 is the root: tree_mask[i, 0] = 1 for every i; tree_mask[i, i] = 1; every other block's ancestors have lower indices than it, and the ancestors of an ancestor are ancestors too. `step_lengths`: some block uses all 256 slots.
All inputs are finite; a program needn't handle non-finite values.
Results may differ from a plain program's by a relative error of at most 0.015.
Values may be sent and summed in bfloat16 or wider, within the bound.
No kernel may reach another device: no remote copies, remote signals or barrier semaphores. Data moves between devices by JAX's collectives and lax.ppermute only.
A program may use at most 64 MiB of HBM per device.

v0:
```python
import math

import jax
import jax.numpy as jnp
from jax import lax
from jax.sharding import PartitionSpec as P

DH = 128
BLOCK = 256


def pick_entry(table, index):
    return jnp.sum(jnp.where(jnp.arange(table.shape[0]) == index, table, 0))


def attend(local_q, keys, values, tree_mask, step_lengths, tile_rows, tile_block):
    rows, qwidth = local_q.shape
    kv_local = keys.shape[1] // DH
    group = qwidth // keys.shape[1]
    nblocks = tree_mask.shape[0]
    ntiles = rows // tile_rows
    scale = 1.0 / math.sqrt(DH)
    query_tiles = local_q.reshape(ntiles, tile_rows, kv_local, group, DH)
    row_pos = jnp.arange(tile_rows)
    tile_onehot = tile_block[:, None] == jnp.arange(nblocks)[None, :]
    start_top = jnp.full((ntiles, tile_rows, kv_local, group), -1e30, jnp.float32)
    start_total = jnp.zeros((ntiles, tile_rows, kv_local, group), jnp.float32)
    start_acc = jnp.zeros((ntiles, tile_rows, kv_local, group, DH), jnp.float32)
    key_piece = lax.all_gather(keys, "seq", axis=0, tiled=True)
    value_piece = lax.all_gather(values, "seq", axis=0, tiled=True)
    count = key_piece.shape[0]
    seg = min(BLOCK, count)

    def one_segment(seg_index, state):
        first = seg_index * seg
        key_block = first // BLOCK
        key_pos = first % BLOCK + jnp.arange(seg)
        key_length = pick_entry(step_lengths, key_block)
        column = jnp.sum(
            jnp.where((jnp.arange(nblocks) == key_block)[None, :], tree_mask, 0), axis=1
        )
        tile_need = jnp.sum(jnp.where(tile_onehot, column[None, :], 0), axis=1) > 0

        def update(current):
            top_old, total_old, acc_old = current
            key_seg = lax.dynamic_slice_in_dim(key_piece, seg_index * seg, seg, 0).reshape(
                seg, kv_local, DH
            )
            value_seg = lax.dynamic_slice_in_dim(value_piece, seg_index * seg, seg, 0).reshape(
                seg, kv_local, DH
            )
            scores = (
                jnp.einsum(
                    "nrkgd,tkd->nrkgt", query_tiles, key_seg, preferred_element_type=jnp.float32
                )
                * scale
            )
            causal = (tile_block != key_block)[:, None, None] | (
                key_pos[None, None, :] <= row_pos[None, :, None]
            )
            allowed = tile_need[:, None, None] & (key_pos < key_length)[None, None, :] & causal
            allowed = allowed[:, :, None, None, :]
            scores = jnp.where(allowed, scores, -1e30)
            top_new = jnp.maximum(top_old, jnp.max(scores, axis=-1))
            weights = jnp.where(allowed, jnp.exp(scores - top_new[..., None]), 0.0)
            factor = jnp.exp(top_old - top_new)
            total_new = total_old * factor + jnp.sum(weights, axis=-1)
            mixed = jnp.einsum(
                "nrkgt,tkd->nrkgd",
                weights.astype(jnp.bfloat16),
                value_seg,
                preferred_element_type=jnp.float32,
            )
            acc_new = acc_old * factor[..., None] + mixed
            return (top_new, total_new, acc_new)

        def unchanged(current):
            return current

        return lax.cond(jnp.any(tile_need), update, unchanged, state)

    top, total, acc = lax.fori_loop(
        0, count // seg, one_segment, (start_top, start_total, start_acc)
    )
    tile_lengths = jnp.sum(jnp.where(tile_onehot, step_lengths[None, :], 0), axis=1)
    valid = row_pos[None, :] < tile_lengths[:, None]
    result = acc / total[..., None]
    result = jnp.where(valid[:, :, None, None, None], result, 0.0)
    return result.reshape(rows, qwidth).astype(jnp.bfloat16)


def on_device(queries, keys, values, tree_mask, step_lengths, probe):
    rows, qwidth = queries.shape
    me_seq = lax.axis_index("seq")
    per_dev = rows // BLOCK
    tile_block = me_seq * per_dev + jnp.arange(per_dev)
    attended = attend(queries, keys, values, tree_mask, step_lengths, BLOCK, tile_block)
    own_blocks = me_seq * per_dev + jnp.arange(per_dev)
    nblocks = tree_mask.shape[0]
    own_lengths = jnp.sum(
        jnp.where(own_blocks[:, None] == jnp.arange(nblocks)[None, :], step_lengths[None, :], 0),
        axis=1,
    )
    last_rows = jnp.arange(per_dev) * BLOCK + own_lengths - 1
    selector = (jnp.arange(rows)[None, :] == last_rows[:, None]).astype(jnp.bfloat16)
    picked = jnp.dot(selector, attended, preferred_element_type=jnp.float32)
    partial_score = jnp.sum(picked * probe.astype(jnp.float32)[None, :], axis=-1)
    step_score = lax.psum(partial_score, "mp")
    return (attended, step_score)


def solution(mesh):
    in_specs = (
        P(("leaf", "seq"), "mp"),
        P(("leaf", "seq"), "mp"),
        P(("leaf", "seq"), "mp"),
        P("leaf", None),
        P("leaf"),
        P("mp"),
    )
    out_specs = (P(("leaf", "seq"), "mp"), P(("leaf", "seq")))
    return jax.shard_map(
        on_device, mesh=mesh, in_specs=in_specs, out_specs=out_specs, check_vma=False
    )
```

profile of v0, /device:TPU:59, one launch (start us, length us, event | category | flops | bytes accessed | tf_op | source)
XLA Modules:
  0.0 278.7 jit_solution(15800274815283477722)
XLA Ops:
  7.2 1.6 copy.13
  8.9 0.7 all-gather.3.cloned.1.call-update
  9.6 1.2 copy.12
  13.0 89.5 %all-gather.5.cloned.1.call-done = bf16[4096,128]{0,1:T(8,128)(2,1)} async-done(((bf16[256,128]{0,1:T(8,128)(2,1)}), bf16[4096,128]{0,1:T(8,128)(2,1)}) %all-gather.5.cloned.1.call-update) | async-done | bytes 1048592 | tf_op jit(solution)/shard_map/all_gather | solution.py:30
  102.5 90.8 %all-gather.3.cloned.1.call-done = bf16[4096,128]{1,0:T(8,128)(2,1)} async-done(((bf16[256,128]{1,0:T(8,128)(2,1)}), bf16[4096,128]{1,0:T(8,128)(2,1)}) %all-gather.3.cloned.1.call-update) | async-done | bytes 1048592 | tf_op jit(solution)/shard_map/all_gather | solution.py:29
  193.4 57.8 %while.20 = (s32[]{:T(128)}, f32[1,256,1,8]{1,3,2,0:T(8,128)S(1)}, f32[1,256,1,8]{1,3,2,0:T(8,128)S(1)}, f32[1,256,1,8,128]{1,4,3,0,2:T(8,128)S(1)}, s32[16,16]{...) while((s32[]{:T(128)}, f32[1,256,1,8]{1,3,2,0:T(8,128)S(1)}, ...), condition=%wide.region_9.10_spmd.clone, body=%wide.region_1.9_spmd.clone.sunk | while | flops 275979648 | bytes 9445043 | solution.py:82
  194.8 5.1 %conditional.3 = ((f32[1,256,1,8]{1,3,2,0:T(8,128)S(1)}, f32[1,256,1,8]{1,3,2,0:T(8,128)S(1)}, f32[1,256,1,8,128]{1,4,3,0,2:T(8,128)S(1)})) conditional(s32[]{:T(128)} %convert_element_type.38, (f32[1,256,1,8]{1,3,2,0:T(8,128)S(1)}, f32[1,256,1,8]{1,3,2,0:T(8,128)S(1)}, f32[1,256,1,8,128]{1,4,3,0,2:T(8,128)S(1)}) %tuple.66, (pred[]{:T(512)}, ...), branch_computations={%region_4.4_spmd, %region_5.8_spmd} | conditional | flops 275979072 | bytes 9442206 | solution.py:80
  194.8 0.7 fusion.22
  196.3 1.3 fusion.4
  197.6 1.7 fusion.7
  201.3 5.1 %conditional.3 = ((f32[1,256,1,8]{1,3,2,0:T(8,128)S(1)}, f32[1,256,1,8]{1,3,2,0:T(8,128)S(1)}, f32[1,256,1,8,128]{1,4,3,0,2:T(8,128)S(1)})) conditional(s32[]{:T(128)} %convert_element_type.38, (f32[1,256,1,8]{1,3,2,0:T(8,128)S(1)}, f32[1,256,1,8]{1,3,2,0:T(8,128)S(1)}, f32[1,256,1,8,128]{1,4,3,0,2:T(8,128)S(1)}) %tuple.66, (pred[]{:T(512)}, ...), branch_computations={%region_4.4_spmd, %region_5.8_spmd} | conditional | flops 275979072 | bytes 9442206 | solution.py:80
  201.3 0.7 fusion.22
  202.8 1.3 fusion.4
  204.1 1.7 fusion.7
  207.8 5.1 %conditional.3 = ((f32[1,256,1,8]{1,3,2,0:T(8,128)S(1)}, f32[1,256,1,8]{1,3,2,0:T(8,128)S(1)}, f32[1,256,1,8,128]{1,4,3,0,2:T(8,128)S(1)})) conditional(s32[]{:T(128)} %convert_element_type.38, (f32[1,256,1,8]{1,3,2,0:T(8,128)S(1)}, f32[1,256,1,8]{1,3,2,0:T(8,128)S(1)}, f32[1,256,1,8,128]{1,4,3,0,2:T(8,128)S(1)}) %tuple.66, (pred[]{:T(512)}, ...), branch_computations={%region_4.4_spmd, %region_5.8_spmd} | conditional | flops 275979072 | bytes 9442206 | solution.py:80
  207.8 0.7 fusion.22
  209.3 1.3 fusion.4
  210.6 1.7 fusion.7
  214.2 5.1 %conditional.3 = ((f32[1,256,1,8]{1,3,2,0:T(8,128)S(1)}, f32[1,256,1,8]{1,3,2,0:T(8,128)S(1)}, f32[1,256,1,8,128]{1,4,3,0,2:T(8,128)S(1)})) conditional(s32[]{:T(128)} %convert_element_type.38, (f32[1,256,1,8]{1,3,2,0:T(8,128)S(1)}, f32[1,256,1,8]{1,3,2,0:T(8,128)S(1)}, f32[1,256,1,8,128]{1,4,3,0,2:T(8,128)S(1)}) %tuple.66, (pred[]{:T(512)}, ...), branch_computations={%region_4.4_spmd, %region_5.8_spmd} | conditional | flops 275979072 | bytes 9442206 | solution.py:80
  215.7 1.3 fusion.4
  217.1 1.7 fusion.7
  224.9 5.1 %conditional.3 = ((f32[1,256,1,8]{1,3,2,0:T(8,128)S(1)}, f32[1,256,1,8]{1,3,2,0:T(8,128)S(1)}, f32[1,256,1,8,128]{1,4,3,0,2:T(8,128)S(1)})) conditional(s32[]{:T(128)} %convert_element_type.38, (f32[1,256,1,8]{1,3,2,0:T(8,128)S(1)}, f32[1,256,1,8]{1,3,2,0:T(8,128)S(1)}, f32[1,256,1,8,128]{1,4,3,0,2:T(8,128)S(1)}) %tuple.66, (pred[]{:T(512)}, ...), branch_computations={%region_4.4_spmd, %region_5.8_spmd} | conditional | flops 275979072 | bytes 9442206 | solution.py:80
  226.4 1.3 fusion.4
  227.7 1.7 fusion.7
  236.9 5.1 %conditional.3 = ((f32[1,256,1,8]{1,3,2,0:T(8,128)S(1)}, f32[1,256,1,8]{1,3,2,0:T(8,128)S(1)}, f32[1,256,1,8,128]{1,4,3,0,2:T(8,128)S(1)})) conditional(s32[]{:T(128)} %convert_element_type.38, (f32[1,256,1,8]{1,3,2,0:T(8,128)S(1)}, f32[1,256,1,8]{1,3,2,0:T(8,128)S(1)}, f32[1,256,1,8,128]{1,4,3,0,2:T(8,128)S(1)}) %tuple.66, (pred[]{:T(512)}, ...), branch_computations={%region_4.4_spmd, %region_5.8_spmd} | conditional | flops 275979072 | bytes 9442206 | solution.py:80
  238.4 1.3 fusion.4
  239.7 1.7 fusion.7
  244.7 5.1 %conditional.3 = ((f32[1,256,1,8]{1,3,2,0:T(8,128)S(1)}, f32[1,256,1,8]{1,3,2,0:T(8,128)S(1)}, f32[1,256,1,8,128]{1,4,3,0,2:T(8,128)S(1)})) conditional(s32[]{:T(128)} %convert_element_type.38, (f32[1,256,1,8]{1,3,2,0:T(8,128)S(1)}, f32[1,256,1,8]{1,3,2,0:T(8,128)S(1)}, f32[1,256,1,8,128]{1,4,3,0,2:T(8,128)S(1)}) %tuple.66, (pred[]{:T(512)}, ...), branch_computations={%region_4.4_spmd, %region_5.8_spmd} | conditional | flops 275979072 | bytes 9442206 | solution.py:80
  246.2 1.3 fusion.4
  247.6 1.7 fusion.7
  251.4 1.0 copy.17
  253.2 18.6 %psum.7 = f32[1]{0:T(128)} all-reduce(f32[1]{0:T(128)} %bitcast.19), channel_id=1, replica_groups=mesh['seq'=16,'mp'=8,'leaf'=4] {'mp'}, use_global_device_ids=true, to_apply=%region_11.12 | all-reduce | flops 1 | bytes 8 | tf_op jit(solution)/shard_map/psum | solution.py:108
  (169 shorter events, 26.4 us)
Async XLA Ops:
  7.2 4.0 %copy-start.1 = (s32[16]{0:T(128)S(1)}, s32[16]{0:T(128)}, u32[]{:S(2)}) copy-start(s32[16]{0:T(128)} %param.14) | copy-start | bytes 196
  7.2 186.3 %copy-start = (s32[16,16]{1,0:T(8,128)S(1)}, s32[16,16]{1,0:T(8,128)}, u32[]{:S(2)}) copy-start(s32[16,16]{1,0:T(8,128)} %param.13) | copy-start | bytes 3076
  7.2 95.3 %all-gather.5.cloned.1.call-start = ((), (), s32[]{:S(2)}) async-start(), calls=%async_computation.1 | async-start | bytes 1114112 | tf_op jit(solution)/shard_map/all_gather | solution.py:30
  8.8 184.5 %all-gather.3.cloned.1.call-start = ((), (), s32[]{:S(2)}) async-start(), calls=%async_computation | async-start | bytes 1114112 | tf_op jit(solution)/shard_map/all_gather | solution.py:29
  251.2 1.4 copy-start.2
Sparse Core Ops, SparseCore 0:
  11.7 90.7 all-gather.4
  105.7 87.5 all-gather.2
where the time goes:
time: 280 us; the launch traced here: 279 us
  waiting for transfers between devices  181 us (65%)
  other arithmetic  27.5 us (10%)
  matrix products  21.4 us (8%)
  blocking collectives  18.6 us (7%)
  between operations  14.7 us (5%)
  loops' own time  11 us (4%)
  local copies, waits for them, and re-layouts  4.34 us (2%)
    all_gather x1, waiting for transfers between devices, attend(): key_piece = lax.all_gather(keys, 'seq', axis=0, tiled=True)  90.8 us
    all_gather x1, waiting for transfers between devices, attend(): value_piece = lax.all_gather(values, 'seq', axis=0, tiled=True)  89.5 us
    psum x1, blocking collectives, on_device(): step_score = lax.psum(partial_score, 'mp')  18.6 us
    dot_general x7, matrix products, update(): jnp.einsum('nrkgt,tkd->nrkgd', weights.astype(jnp.bfloat16), value_seg, p...  12 us
    another operation x1, loops' own time, attend(): lax.fori_loop(0, count // seg, one_segment, (start_top, start_total, star...  10.2 us
    reduce_sum x16, other arithmetic, one_segment(): tile_need = jnp.sum(jnp.where(tile_onehot, column[None, :], 0), axis=1) > 0  9.74 us
    dot_general x7, matrix products, update(): jnp.einsum('nrkgd,tkd->nrkgt', query_tiles, key_seg, preferred_element_ty...  9.14 us
  transfers between devices with their start and end apart: 2, of which 2 were waited for; matrix products, arithmetic and copies ran while one was open for 1% of the time, Pallas kernels for 0%

commit v1 on v0

v1 whole, which is shorter than its diff:
```python
import functools
import math

import jax
import jax.numpy as jnp
from jax import lax
from jax.experimental import pallas as pl
from jax.experimental.pallas import tpu as pltpu
from jax.sharding import PartitionSpec as P

DH = 128
BLOCK = 256
CHUNK = 16
PAIR = 2 * CHUNK
NEG = -1e30

VMEM = pltpu.VMEM
SMEM = pltpu.SMEM


def chunks_of(length):
    return (length + CHUNK - 1) // CHUNK


def plan_kernel(planes, sizes, mask_ref, len_ref, k_ref, v_ref, send_ref, meta_ref):
    nblocks = mask_ref.shape[0]
    holders = nblocks // planes
    me = lax.axis_index("seq")
    counts = [chunks_of(len_ref[b]) for b in range(nblocks)]
    most = jnp.int32(0)
    my_start = jnp.int32(0)
    for b in range(nblocks):
        for plane in range(planes):
            total = jnp.int32(0)
            for a in range(plane, b, planes):
                total += jnp.where(mask_ref[b, a] > 0, counts[a], 0)
            most = jnp.maximum(most, total)
            if plane == b % planes:
                meta_ref[b] = total
                my_start = jnp.where(me == b, total, my_start)
    slots = (most + holders - 1) // holders
    choice = jnp.int32(0)
    for size in sizes[:-1]:
        choice += jnp.where(slots > size, 1, 0)
    meta_ref[nblocks] = choice
    per = BLOCK // CHUNK // holders
    for chunk in range(BLOCK // CHUNK):
        holder = lax.rem(my_start + chunk, holders)
        row = (chunk // holders) * PAIR
        rows = slice(chunk * CHUNK, (chunk + 1) * CHUNK)
        send_ref[holder, row : row + CHUNK, :] = k_ref[rows, :]
        send_ref[holder, row + CHUNK : row + PAIR, :] = v_ref[rows, :]


def pack_kernel(planes, slots, mask_ref, len_ref, meta_ref, held_ref, send_ref):
    nblocks = mask_ref.shape[0]
    holders = nblocks // planes
    me = lax.axis_index("seq")
    mine, plane = me // planes, lax.rem(me, planes)
    send_ref[...] = jnp.zeros_like(send_ref)
    for y in range(holders):
        block = y * planes + plane
        start = meta_ref[block]
        count = chunks_of(len_ref[block])
        first = lax.rem(mine - start + BLOCK, holders)
        for k in range(BLOCK // CHUNK // holders):
            chunk = first + k * holders
            row = pl.multiple_of((start + chunk) // holders * PAIR, PAIR)

            @pl.when(chunk < count)
            def _():
                piece = held_ref[y, k * PAIR : (k + 1) * PAIR, :]
                for j in range(y * planes + 1, nblocks):

                    @pl.when((mask_ref[j, block] > 0) & (block < j))
                    def _():
                        send_ref[j, pl.ds(row, PAIR), :] = piece


def attend_kernel(
    planes, slots, mask_ref, len_ref, meta_ref, q_ref, k_ref, v_ref, got_ref, probe_ref, out_ref, score_ref,
    keys, vals, bias,
):
    nblocks = mask_ref.shape[0]
    me = lax.axis_index("seq")
    length = len_ref[me]
    scale = 1.0 / math.sqrt(DH)
    width = nblocks * CHUNK
    lane = lax.broadcasted_iota(jnp.int32, (slots, width), 1)
    slot = lax.broadcasted_iota(jnp.int32, (slots, width), 0)
    source = lane // CHUNK
    where_row = (slot * (nblocks // planes) + source // planes) * CHUNK + lane % CHUNK
    of_plane = source % planes
    allowed = jnp.zeros((slots, width), jnp.bool_)
    for b in range(nblocks - 1):
        used = jnp.where((mask_ref[me, b] > 0) & (b != me), len_ref[b], 0)
        row = where_row - meta_ref[b] * CHUNK
        allowed |= (of_plane == b % planes) & (row >= 0) & (row < used)
    bias[...] = jnp.where(allowed, 0.0, NEG)
    for s in range(slots):
        for i in range(nblocks):
            at = s * width + i * CHUNK
            keys[at : at + CHUNK, :] = got_ref[i, s * PAIR : s * PAIR + CHUNK, :]
            vals[at : at + CHUNK, :] = got_ref[i, s * PAIR + CHUNK : (s + 1) * PAIR, :]
    row_id = lax.broadcasted_iota(jnp.int32, (BLOCK, 1), 0)
    causal = lax.broadcasted_iota(jnp.int32, (BLOCK, BLOCK), 1) <= row_id
    nt = (((1,), (1,)), ((), ()))
    nheads = q_ref.shape[1] // DH

    def one_head(h, carry):
        columns = pl.ds(pl.multiple_of(h * DH, DH), DH)
        q = q_ref[:, columns]
        own = lax.dot_general(q, k_ref[...], nt, preferred_element_type=jnp.float32)
        parts = [jnp.where(causal, own, NEG)]
        for s in range(slots):
            part = lax.dot_general(
                q, keys[s * width : (s + 1) * width, :], nt, preferred_element_type=jnp.float32
            )
            parts.append(part + bias[s : s + 1, :])
        top = functools.reduce(jnp.maximum, [jnp.max(p, axis=1, keepdims=True) for p in parts])
        total = jnp.zeros((BLOCK, 1), jnp.float32)
        acc = jnp.zeros((BLOCK, DH), jnp.float32)
        for n, part in enumerate(parts):
            w = jnp.exp((part - top) * scale)
            total += jnp.sum(w, axis=1, keepdims=True)
            v = v_ref[...] if n == 0 else vals[(n - 1) * width : n * width, :]
            acc += jnp.dot(w.astype(jnp.bfloat16), v, preferred_element_type=jnp.float32)
        out_ref[:, columns] = jnp.where(row_id < length, acc / total, 0.0).astype(out_ref.dtype)
        return carry

    lax.fori_loop(0, nheads, one_head, 0)
    last = length - 1
    base = pl.multiple_of(last // CHUNK * CHUNK, CHUNK)
    rows = out_ref[pl.ds(base, CHUNK), :].astype(jnp.float32)
    picked = lax.broadcasted_iota(jnp.int32, (CHUNK, 1), 0) == last - base
    part = jnp.where(picked, rows, 0.0) * probe_ref[...].astype(jnp.float32)
    score_ref[...] = jnp.full(score_ref.shape, jnp.sum(part), jnp.float32)


def on_device(planes, queries, keys, values, tree_mask, step_lengths, probe):
    nblocks = tree_mask.shape[0]
    holders = nblocks // planes
    sizes = [s for s in (2, 3, 4, 5, 6, 7, 8, 10, 12, 16)]
    smem, vmem = pl.BlockSpec(memory_space=SMEM), pl.BlockSpec(memory_space=VMEM)
    per = BLOCK // CHUNK // holders
    send, meta = pl.pallas_call(
        functools.partial(plan_kernel, planes, sizes),
        out_shape=(
            jax.ShapeDtypeStruct((holders, per * PAIR, DH), jnp.bfloat16),
            jax.ShapeDtypeStruct((nblocks + 1,), jnp.int32),
        ),
        in_specs=[smem, smem, vmem, vmem],
        out_specs=(vmem, smem),
    )(tree_mask, step_lengths, keys, values)
    groups = [[y * planes + p for y in range(holders)] for p in range(planes)]
    held = lax.all_to_all(send, "seq", 0, 0, axis_index_groups=groups)

    def rest(slots, held, meta):
        packed = pl.pallas_call(
            functools.partial(pack_kernel, planes, slots),
            out_shape=jax.ShapeDtypeStruct((nblocks, slots * PAIR, DH), jnp.bfloat16),
            in_specs=[smem, smem, smem, vmem],
            out_specs=vmem,
        )(tree_mask, step_lengths, meta, held)
        got = lax.all_to_all(packed, "seq", 0, 0)
        rows = slots * nblocks * CHUNK
        return pl.pallas_call(
            functools.partial(attend_kernel, planes, slots),
            out_shape=(
                jax.ShapeDtypeStruct(queries.shape, jnp.bfloat16),
                jax.ShapeDtypeStruct((8, 1, 128), jnp.float32),
            ),
            in_specs=[smem, smem, smem, vmem, vmem, vmem, vmem, vmem],
            out_specs=(vmem, vmem),
            scratch_shapes=[
                VMEM((rows, DH), jnp.bfloat16),
                VMEM((rows, DH), jnp.bfloat16),
                VMEM((slots, nblocks * CHUNK), jnp.float32),
            ],
            compiler_params=pltpu.CompilerParams(vmem_limit_bytes=48 * 1024 * 1024),
        )(tree_mask, step_lengths, meta, queries, keys, values, got, probe.reshape(1, -1))

    branches = [functools.partial(rest, s) for s in sizes]
    attended, score = lax.switch(meta[nblocks], branches, held, meta)
    parts = lax.all_to_all(score, "mp", 0, 0)
    return attended, jnp.sum(parts[:, 0, :1], axis=0)


def solution(mesh):
    in_specs = (
        P(("leaf", "seq"), "mp"),
        P(("leaf", "seq"), "mp"),
        P(("leaf", "seq"), "mp"),
        P("leaf", None),
        P("leaf"),
        P("mp"),
    )
    out_specs = (P(("leaf", "seq"), "mp"), P(("leaf", "seq")))
    return jax.shard_map(
        functools.partial(on_device, 2), mesh=mesh, in_specs=in_specs, out_specs=out_specs, check_vma=False
    )
```

time: 280 us -> 75.1 us (0.27)
  the two profiles are of different devices: /device:TPU:59 before, /device:TPU:1 now
where the time goes in v1:
time: 75.1 us; the launch traced here: 74.6 us
  waiting for transfers between devices  30.6 us (41%)
  starting transfers between devices  17.9 us (24%)
  Pallas kernels  13.1 us (17%)
  blocking collectives  10.5 us (14%)
  between operations  1.29 us (2%)
    all_to_all x1, waiting for transfers between devices, rest(): got = lax.all_to_all(packed, 'seq', 0, 0)  23.8 us
    all_to_all x1, blocking collectives, on_device(): parts = lax.all_to_all(score, 'mp', 0, 0)  10.5 us
    all_to_all x1, starting transfers between devices, rest(): got = lax.all_to_all(packed, 'seq', 0, 0)  10.3 us
    pallas_call x1, Pallas kernels, rest(): pl.pallas_call(functools.partial(attend_kernel, planes, slots), out_shape...  8.34 us
    all_to_all x1, starting transfers between devices, on_device(): held = lax.all_to_all(send, 'seq', 0, 0, axis_index_groups=groups)  7.66 us
    all_to_all x1, waiting for transfers between devices, on_device(): held = lax.all_to_all(send, 'seq', 0, 0, axis_index_groups=groups)  6.79 us
    pallas_call x1, Pallas kernels, rest(): pl.pallas_call(functools.partial(pack_kernel, planes, slots), out_shape=j...  2.93 us
    pallas_call x1, Pallas kernels, on_device(): pl.pallas_call(functools.partial(plan_kernel, planes, sizes), out_shape=(...  1.8 us
  transfers between devices with their start and end apart: 2, of which 2 were waited for; matrix products, arithmetic and copies ran while one was open for 1% of the time, Pallas kernels for 0%

profile of v1, /device:TPU:1, one launch (start us, length us, event | category | flops | bytes accessed | tf_op | source)
XLA Modules:
  0.0 74.6 jit_solution(8806310442846246314)
XLA Ops:
  0.6 1.8 %shard_map.77 = (bf16[8,64,128]{2,1,0:T(8,128)(2,1)}, s32[17]{0:T(128)S(1)}) custom-call(s32[16,16]{1,0:T(8,128)} %mask_ref.1, s32[16]{0:T(128)} %len_ref.1, bf16[256,128]{1,0:T(8,128)(2,1)} %k_ref.1, bf16[256,128]{1,0:T(8,128)(2,1)} %v_ref.1), custom_call_target="tpu_custom_call" | custom-call | tf_op jit(solution)/shard_map/pallas_call | solution.py:146
  2.4 7.7 %all-to-all-start.10 = ((bf16[8,64,128]{2,1,0:T(8,128)(2,1)}), bf16[8,64,128]{2,1,0:T(8,128)(2,1)S(1)}, u32[]{:S(2)}, u32[]{:S(2)}) async-start(bf16[8,64,128]{2,1,0:T(8,128)(2,1)} %get-tuple-element.247), calls=%async_computation.10 | async-start | bytes 262144 | tf_op jit(solution)/shard_map/all_to_all | solution.py:156
  10.1 0.6 slice.6
  11.3 6.8 %all-to-all-done.10 = bf16[8,64,128]{2,1,0:T(8,128)(2,1)S(1)} async-done(((bf16[8,64,128]{2,1,0:T(8,128)(2,1)}), bf16[8,64,128]{2,1,0:T(8,128)(2,1)S(1)}, u32[]{:S(2)}, u32[]{:S(2)}) %all-to-all-start.10) | async-done | bytes 131104 | tf_op jit(solution)/shard_map/all_to_all | solution.py:156
  18.1 45.4 %conditional.1 = ((bf16[256,1024]{1,0:T(8,128)(2,1)}, f32[8,1,128]{2,1,0:T(1,128)S(1)})) conditional(s32[]{:T(128)} %bitcast, (s32[16,16]{1,0:T(8,128)}, s32[16]{0:T(128)}, s32[17]{0:T(128)S(1)}, bf16[8,64,128]{2,1,0:T(8,128)(2,1)S(1)}, bf16[1024]{0:T(1024)(128)(2,1)}, /*index=5*/bf16[256,1024]{1,0:T(8,128)(2,1)}, ...), branch_computations={%region_0.0_spmd, %region_1.0_spmd, %region_2.0_spmd, %region_3.0_... | conditional | bytes 8929744 | solution.py:184
  18.1 0.0 copy-start.42
  18.1 0.0 copy-start.2
  18.1 0.0 copy-start.10
  18.1 0.0 copy-start.18
  18.1 0.0 copy-start.26
  18.2 0.0 copy-start.34
  18.2 2.9 %branch_3_fun.2 = bf16[16,160,128]{2,1,0:T(8,128)(2,1)} custom-call(s32[16,16]{1,0:T(8,128)} %get-tuple-element.184.mask_ref, s32[16]{0:T(128)} %get-tuple-element.185.len_ref, s32[17]{0:T(128)S(1)} %get-tuple-element.186.meta_ref, bf16[8,64,128]{2,1,0:T(8,128)(2,1)S(1)} %get-tuple-element.190.held_ref), custom_call_target="tpu_custom_call" | custom-call | tf_op jit(solution)/shard_map/cond/branch_3_fun/pallas_call | solution.py:159
  21.1 10.3 %all-to-all-start.3 = ((bf16[16,160,128]{2,1,0:T(8,128)(2,1)}), bf16[16,160,128]{2,1,0:T(8,128)(2,1)S(1)}, u32[]{:S(2)}, u32[]{:S(2)}) async-start(bf16[16,160,128]{2,1,0:T(8,128)(2,1)} %branch_3_fun.2), calls=%async_computation.3 | async-start | bytes 1310720 | tf_op jit(solution)/shard_map/cond/branch_3_fun/all_to_all | solution.py:165
  31.4 0.0 copy-done.42
  31.4 23.8 %all-to-all-done.3.got_ref = bf16[16,160,128]{2,1,0:T(8,128)(2,1)S(1)} async-done(((bf16[16,160,128]{2,1,0:T(8,128)(2,1)}), bf16[16,160,128]{2,1,0:T(8,128)(2,1)S(1)}, u32[]{:S(2)}, u32[]{:S(2)}) %all-to-all-start.3) | async-done | bytes 655392 | tf_op jit(solution)/shard_map/cond/branch_3_fun/all_to_all | solution.py:165
  55.2 0.0 copy-done.2
  55.2 0.0 copy-done.10
  55.2 0.0 copy-done.18
  55.2 0.0 copy-done.26
  55.2 0.0 copy-done.34
  55.2 8.3 %branch_3_fun.3 = (bf16[256,1024]{1,0:T(8,128)(2,1)}, f32[8,1,128]{2,1,0:T(1,128)S(1)}) custom-call(s32[16,16]{1,0:T(8,128)S(1)} %copy-done.26, s32[16]{0:T(128)S(1)} %copy-done.34, s32[17]{0:T(128)S(1)} %get-tuple-element.186.meta_ref, bf16[256,1024]{1,0:T(8,128)(2,1)S(1)} %copy-done.2, bf16[256,128]{1,0:T(8,128)(2,1)S(1)} %copy-done.10, ...), custom_call_target="tpu_custom_call" | custom-call | tf_op jit(solution)/shard_map/cond/branch_3_fun/pallas_call | solution.py:167
  63.5 10.5 %all_to_all.50 = f32[8,1,128]{2,1,0:T(1,128)S(1)} all-to-all(f32[8,1,128]{2,1,0:T(1,128)S(1)} %get-tuple-element.249), channel_id=1, replica_groups=mesh['seq'=16,'mp'=8,'leaf'=4] {'mp'}, dimensions={0} | all-to-all | bytes 8192 | tf_op jit(solution)/shard_map/all_to_all | solution.py:185
  74.0 0.6 slice_reduce_fusion
  (1 shorter events, 0.0 us)
Async XLA Ops:
  2.4 15.7 %all-to-all-start.10 = ((bf16[8,64,128]{2,1,0:T(8,128)(2,1)}), bf16[8,64,128]{2,1,0:T(8,128)(2,1)S(1)}, u32[]{:S(2)}, u32[]{:S(2)}) async-start(bf16[8,64,128]{2,1,0:T(8,128)(2,1)} %get-tuple-element.247), calls=%async_computation.10 | async-start | bytes 262144 | tf_op jit(solution)/shard_map/all_to_all | solution.py:156
  18.1 13.3 %copy-start.42 = (bf16[1024]{0:T(1024)(128)(2,1)S(1)}, bf16[1024]{0:T(1024)(128)(2,1)}, u32[]{:S(2)}) copy-start(bf16[1024]{0:T(1024)(128)(2,1)} %get-tuple-element.191) | copy-start | bytes 6148 | tf_op jit(solution)/shard_map/cond
  18.1 37.0 %copy-start.2 = (bf16[256,1024]{1,0:T(8,128)(2,1)S(1)}, bf16[256,1024]{1,0:T(8,128)(2,1)}, u32[]{:S(2)}) copy-start(bf16[256,1024]{1,0:T(8,128)(2,1)} %get-tuple-element.187.q_ref) | copy-start | bytes 1572868 | tf_op jit(solution)/shard_map/cond
  18.1 37.0 %copy-start.10 = (bf16[256,128]{1,0:T(8,128)(2,1)S(1)}, bf16[256,128]{1,0:T(8,128)(2,1)}, u32[]{:S(2)}) copy-start(bf16[256,128]{1,0:T(8,128)(2,1)} %get-tuple-element.188.k_ref) | copy-start | bytes 196612 | tf_op jit(solution)/shard_map/cond
  18.1 37.0 %copy-start.18 = (bf16[256,128]{1,0:T(8,128)(2,1)S(1)}, bf16[256,128]{1,0:T(8,128)(2,1)}, u32[]{:S(2)}) copy-start(bf16[256,128]{1,0:T(8,128)(2,1)} %get-tuple-element.189.v_ref) | copy-start | bytes 196612 | tf_op jit(solution)/shard_map/cond
  18.1 37.0 %copy-start.26 = (s32[16,16]{1,0:T(8,128)S(1)}, s32[16,16]{1,0:T(8,128)}, u32[]{:S(2)}) copy-start(s32[16,16]{1,0:T(8,128)} %get-tuple-element.184.mask_ref) | copy-start | bytes 3076 | tf_op jit(solution)/shard_map/cond
  18.2 37.0 %copy-start.34 = (s32[16]{0:T(128)S(1)}, s32[16]{0:T(128)}, u32[]{:S(2)}) copy-start(s32[16]{0:T(128)} %get-tuple-element.185.len_ref) | copy-start | bytes 196 | tf_op jit(solution)/shard_map/cond
  21.1 34.1 %all-to-all-start.3 = ((bf16[16,160,128]{2,1,0:T(8,128)(2,1)}), bf16[16,160,128]{2,1,0:T(8,128)(2,1)S(1)}, u32[]{:S(2)}, u32[]{:S(2)}) async-start(bf16[16,160,128]{2,1,0:T(8,128)(2,1)} %branch_3_fun.2), calls=%async_computation.3 | async-start | bytes 1310720 | tf_op jit(solution)/shard_map/cond/branch_3_fun/all_to_all | solution.py:165

commit v2 on v1

v2 whole, which is shorter than its diff:
```python
import functools
import math

import jax
import jax.numpy as jnp
from jax import lax
from jax.experimental import pallas as pl
from jax.experimental.pallas import tpu as pltpu
from jax.sharding import PartitionSpec as P

DH = 128
BLOCK = 256
CHUNK = 16
PAIR = 2 * CHUNK
PER_KEYS = BLOCK // CHUNK
NEG = -1e30
NT = (((1,), (1,)), ((), ()))
SIZES = (3, 4, 5, 6, 7, 8, 11, 16)

VMEM = pltpu.VMEM
SMEM = pltpu.SMEM


def chunks_of(length):
    return (length + CHUNK - 1) // CHUNK


def spread_kernel(planes, mask_ref, len_ref, k_ref, v_ref, send_ref):
    nblocks = mask_ref.shape[0]
    holders = nblocks // planes
    me = lax.axis_index("seq")
    start = jnp.int32(0)
    for a in range(nblocks - 1):
        counted = (a < me) & (lax.rem(me, planes) == a % planes)
        start += jnp.where(counted, mask_ref[me, a] * chunks_of(len_ref[a]), 0)
    for chunk in range(PER_KEYS):
        holder = lax.rem(start + chunk, holders)
        row = (chunk // holders) * PAIR
        rows = slice(chunk * CHUNK, (chunk + 1) * CHUNK)
        send_ref[holder, row : row + CHUNK, :] = k_ref[rows, :]
        send_ref[holder, row + CHUNK : row + PAIR, :] = v_ref[rows, :]


def table_kernel(planes, mask_ref, len_ref, meta_ref, choice_ref):
    nblocks = mask_ref.shape[0]
    holders = nblocks // planes
    me = lax.axis_index("seq")
    counts = [chunks_of(len_ref[b]) for b in range(nblocks)]
    most = jnp.int32(0)
    mine = [jnp.int32(0) for _ in range(planes)]
    for b in range(nblocks):
        for plane in range(planes):
            total = jnp.int32(0)
            for a in range(plane, b, planes):
                total += mask_ref[b, a] * counts[a]
            most = jnp.maximum(most, total)
            mine[plane] = jnp.where(me == b, total, mine[plane])
            if plane == b % planes:
                meta_ref[b] = total
    for plane in range(planes):
        meta_ref[nblocks + plane] = mine[plane]
    slots = (most + holders - 1) // holders
    choice = jnp.int32(0)
    for size in SIZES[:-1]:
        choice += jnp.where(slots > size, 1, 0)
    choice_ref[0] = choice


def pack_kernel(planes, slots, mask_ref, len_ref, meta_ref, held_ref, send_ref, work):
    nblocks = mask_ref.shape[0]
    holders = nblocks // planes
    me = lax.axis_index("seq")
    mine, plane = me // planes, lax.rem(me, planes)
    work[...] = jnp.zeros_like(work)

    for y in range(holders):
        block = y * planes + plane
        start = meta_ref[block]
        count = chunks_of(len_ref[block])
        first = lax.rem(mine - start + BLOCK, holders)
        for k in range(PER_KEYS // holders):
            chunk = first + k * holders
            slot = jnp.minimum((start + chunk) // holders, slots - 1)
            row = pl.multiple_of(slot * PAIR, PAIR)
            used = jnp.where(chunk < count, 1, 0)
            piece = held_ref[y, k * PAIR : (k + 1) * PAIR, :]
            for j in range(y * planes + 1, nblocks):
                needed = mask_ref[j, block] * used
                if j < (y + 1) * planes:
                    needed = jnp.where(block < j, needed, 0)
                work[jnp.where(needed > 0, j, nblocks), pl.ds(row, PAIR), :] = piece
    send_ref[...] = work[:nblocks]


def own_kernel(
    planes, slots, mask_ref, len_ref, meta_ref, q_ref, k_ref, v_ref, probe_ref,
    top_ref, total_ref, acc_ref, across_ref, down_ref, lastq_ref, probes_ref, own_s_ref, own_p_ref, vt,
):
    nblocks = mask_ref.shape[0]
    me = lax.axis_index("seq")
    length = len_ref[me]
    nheads = q_ref.shape[1] // DH
    scale = 1.0 / math.sqrt(DH)
    row_at = lax.broadcasted_iota(jnp.int32, (slots, BLOCK), 0) * BLOCK
    row_at = row_at + lax.broadcasted_iota(jnp.int32, (slots, BLOCK), 1)
    row_id = lax.broadcasted_iota(jnp.int32, (CHUNK, DH), 0)
    allowed = jnp.zeros((slots, BLOCK), jnp.int32)
    down_ref[...] = jnp.full(down_ref.shape, NEG, jnp.float32)
    for b in range(nblocks - 1):
        before = meta_ref[b]
        for plane in range(b % planes):
            before += meta_ref[nblocks + plane]
        used = jnp.where((mask_ref[me, b] > 0) & (b < me), len_ref[b], 0)
        row = row_at - before * CHUNK
        allowed = jnp.where((row >= 0) & (row < used), 1, allowed)

        def one_chunk(c, carry):
            at = pl.multiple_of((before + c) * CHUNK, CHUNK)
            down_ref[pl.ds(at, CHUNK), :] = jnp.where(row_id < used - c * CHUNK, 0.0, NEG)
            return carry

        lax.fori_loop(0, chunks_of(used), one_chunk, 0)
    across_ref[...] = jnp.where(allowed > 0, 0.0, NEG)
    causal = lax.broadcasted_iota(jnp.int32, (BLOCK, BLOCK), 0) <= lax.broadcasted_iota(
        jnp.int32, (BLOCK, BLOCK), 1
    )
    vt[...] = jnp.transpose(v_ref[...].astype(jnp.float32)).astype(jnp.bfloat16)
    last = length - 1
    base = pl.multiple_of(last // CHUNK * CHUNK, CHUNK)
    picked = lax.broadcasted_iota(jnp.int32, (CHUNK, 1), 0) == last - base

    def one_head(h, carry):
        columns = pl.ds(pl.multiple_of(h * DH, DH), DH)
        scores = lax.dot_general(k_ref[...], q_ref[:, columns], NT, preferred_element_type=jnp.float32)
        scores = jnp.where(causal, scores, NEG)
        top = jnp.max(scores, axis=0, keepdims=True)
        w = jnp.exp((scores - top) * scale)
        top_ref[h] = top
        total_ref[h] = jnp.sum(w, axis=0, keepdims=True)
        acc_ref[h] = jnp.dot(vt[...], w.astype(jnp.bfloat16), preferred_element_type=jnp.float32)
        return carry

    lax.fori_loop(0, nheads, one_head, 0)
    for h in range(nheads):
        columns = slice(h * DH, (h + 1) * DH)
        near = q_ref[pl.ds(base, CHUNK), columns].astype(jnp.float32)
        lastq_ref[h : h + 1, :] = jnp.sum(jnp.where(picked, near, 0.0), axis=0, keepdims=True)
        probes_ref[h : h + 1, :] = probe_ref[:, columns].astype(jnp.float32)
    lastq = lastq_ref[...].astype(jnp.bfloat16)
    probes = probes_ref[...].astype(jnp.bfloat16)
    own_s = lax.dot_general(lastq, k_ref[...], NT, preferred_element_type=jnp.float32)
    inside = lax.broadcasted_iota(jnp.int32, (1, BLOCK), 1) < length
    own_s_ref[...] = jnp.where(inside, own_s, NEG)
    own_p_ref[...] = lax.dot_general(probes, v_ref[...], NT, preferred_element_type=jnp.float32)


def score_kernel(
    planes, slots, meta_ref, got_ref, across_ref, lastq_ref, probes_ref, own_s_ref, own_p_ref, score_ref, keys_ref, vals_ref,
):
    nblocks = got_ref.shape[0]
    holders = nblocks // planes
    scale = 1.0 / math.sqrt(DH)
    zeros = jnp.zeros((BLOCK, DH), jnp.bfloat16)
    before = jnp.int32(0)
    for plane in range(planes):
        tail = pl.multiple_of((before + slots * holders) * CHUNK, CHUNK)
        if plane == 0:
            keys_ref[slots * holders * CHUNK :, :] = jnp.zeros_like(keys_ref[slots * holders * CHUNK :, :])
            vals_ref[slots * holders * CHUNK :, :] = jnp.zeros_like(vals_ref[slots * holders * CHUNK :, :])
        else:
            keys_ref[pl.ds(tail, BLOCK), :] = zeros
            vals_ref[pl.ds(tail, BLOCK), :] = zeros
        for s in range(slots):
            for p in range(holders):
                at = pl.multiple_of((before + s * holders + p) * CHUNK, CHUNK)
                i = p * planes + plane
                keys_ref[pl.ds(at, CHUNK), :] = got_ref[i, s * PAIR : s * PAIR + CHUNK, :]
                vals_ref[pl.ds(at, CHUNK), :] = got_ref[i, s * PAIR + CHUNK : (s + 1) * PAIR, :]
        before += meta_ref[nblocks + plane]
    lastq = lastq_ref[...].astype(jnp.bfloat16)
    probes = probes_ref[...].astype(jnp.bfloat16)
    scores, products = [own_s_ref[...]], [own_p_ref[...]]
    for s in range(slots):
        rows = slice(s * BLOCK, (s + 1) * BLOCK)
        part = lax.dot_general(lastq, keys_ref[rows, :], NT, preferred_element_type=jnp.float32)
        scores.append(part + across_ref[s : s + 1, :])
        products.append(
            lax.dot_general(probes, vals_ref[rows, :], NT, preferred_element_type=jnp.float32)
        )
    top = jnp.max(functools.reduce(jnp.maximum, scores), axis=1, keepdims=True)
    weights = [jnp.exp((part - top) * scale) for part in scores]
    total = jnp.sum(sum(weights), axis=1, keepdims=True)
    mixed = jnp.sum(sum(w * p for w, p in zip(weights, products)), axis=1, keepdims=True)
    score_ref[...] = jnp.full(score_ref.shape, jnp.sum(mixed / total), jnp.float32)


def attend_kernel(
    planes, slots, len_ref, meta_ref, q_ref, keys_ref, vals_ref, down_ref, top_ref, total_ref, acc_ref, out_ref,
    kept, tops, totals, accs,
):
    length = len_ref[lax.axis_index("seq")]
    nblocks = len_ref.shape[0]
    nheads = q_ref.shape[1] // DH
    scale = 1.0 / math.sqrt(DH)
    count = jnp.int32(0)
    for plane in range(planes):
        count += meta_ref[nblocks + plane]
    steps = (count + PER_KEYS - 1) // PER_KEYS
    for h in range(nheads):
        tops[h] = jnp.broadcast_to(top_ref[h], (8, BLOCK))

    def one_score(n, carry):
        at = pl.ds(pl.multiple_of(n * BLOCK, BLOCK), BLOCK)
        bias = down_ref[at, :]
        bias = jnp.concatenate([bias, bias], axis=1)
        for h in range(nheads):
            q = q_ref[:, h * DH : (h + 1) * DH]
            part = lax.dot_general(keys_ref[at, :], q, NT, preferred_element_type=jnp.float32) + bias
            kept[n, h] = part
            tops[h] = jnp.maximum(tops[h], jnp.max(part.reshape(BLOCK // 8, 8, BLOCK), axis=0))
        return carry

    lax.fori_loop(0, steps, one_score, 0)
    for h in range(nheads):
        top = jnp.max(tops[h], axis=0, keepdims=True)
        tops[h] = jnp.broadcast_to(top, (8, BLOCK))
        factor = jnp.exp((top_ref[h] - top) * scale)
        row = lax.broadcasted_iota(jnp.int32, (8, BLOCK), 0)
        totals[h] = jnp.where(row == 0, total_ref[h] * factor, 0.0)
        accs[h] = acc_ref[h] * factor

    def one_mix(n, carry):
        at = pl.ds(pl.multiple_of(n * BLOCK, BLOCK), BLOCK)
        vt = jnp.transpose(vals_ref[at, :].astype(jnp.float32)).astype(jnp.bfloat16)
        for h in range(nheads):
            w = jnp.exp((kept[n, h] - tops[h, :1, :]) * scale)
            totals[h] += jnp.sum(w.reshape(BLOCK // 8, 8, BLOCK), axis=0)
            accs[h] += jnp.dot(vt, w.astype(jnp.bfloat16), preferred_element_type=jnp.float32)
        return carry

    lax.fori_loop(0, steps, one_mix, 0)
    row_id = lax.broadcasted_iota(jnp.int32, (BLOCK, 1), 0)
    for h in range(nheads):
        total = jnp.sum(totals[h], axis=0, keepdims=True)
        result = jnp.transpose(accs[h] / total)
        out_ref[:, h * DH : (h + 1) * DH] = jnp.where(row_id < length, result, 0.0).astype(out_ref.dtype)


def on_device(planes, queries, keys, values, tree_mask, step_lengths, probe):
    nblocks = tree_mask.shape[0]
    holders = nblocks // planes
    nheads = queries.shape[1] // DH
    smem, vmem = pl.BlockSpec(memory_space=SMEM), pl.BlockSpec(memory_space=VMEM)
    f32, bf16 = jnp.float32, jnp.bfloat16
    shape = jax.ShapeDtypeStruct
    limit = lambda mib: pltpu.CompilerParams(vmem_limit_bytes=mib * 1024 * 1024)
    send = pl.pallas_call(
        functools.partial(spread_kernel, planes),
        out_shape=shape((holders, PER_KEYS // holders * PAIR, DH), bf16),
        in_specs=[smem, smem, vmem, vmem],
        out_specs=vmem,
        compiler_params=limit(8),
    )(tree_mask, step_lengths, keys, values)
    groups = [[y * planes + p for y in range(holders)] for p in range(planes)]
    held = lax.all_to_all(send, "seq", 0, 0, axis_index_groups=groups)
    meta, choice = pl.pallas_call(
        functools.partial(table_kernel, planes),
        out_shape=(shape((nblocks + planes,), jnp.int32), shape((1,), jnp.int32)),
        in_specs=[smem, smem],
        out_specs=(smem, smem),
        cost_estimate=pl.CostEstimate(flops=10**8, bytes_accessed=10**5, transcendentals=0),
        compiler_params=limit(8),
    )(tree_mask, step_lengths)

    def rest(slots, held, meta):
        packed = pl.pallas_call(
            functools.partial(pack_kernel, planes, slots),
            out_shape=shape((nblocks, slots * PAIR, DH), bf16),
            in_specs=[smem, smem, smem, vmem],
            out_specs=vmem,
            scratch_shapes=[VMEM((nblocks + 1, slots * PAIR, DH), bf16)],
            compiler_params=limit(16),
        )(tree_mask, step_lengths, meta, held)
        got = lax.all_to_all(packed, "seq", 0, 0)
        per_head = shape((nheads, 1, BLOCK), f32)
        small = shape((nheads, DH), f32)
        top, total, acc, across, down, lastq, probes, own_s, own_p = pl.pallas_call(
            functools.partial(own_kernel, planes, slots),
            out_shape=(
                per_head, per_head, shape((nheads, DH, BLOCK), f32), shape((slots, BLOCK), f32),
                shape((slots * BLOCK, DH), f32), small, small,
                shape((nheads, BLOCK), f32), shape((nheads, BLOCK), f32),
            ),
            in_specs=[smem, smem, smem, vmem, vmem, vmem, vmem],
            out_specs=(vmem,) * 9,
            scratch_shapes=[VMEM((DH, BLOCK), bf16)],
            cost_estimate=pl.CostEstimate(flops=10**9, bytes_accessed=5 * 10**6, transcendentals=10**6),
            compiler_params=limit(12),
        )(tree_mask, step_lengths, meta, queries, keys, values, probe.reshape(1, -1))
        together = shape((slots * BLOCK + BLOCK, DH), bf16)
        score, all_keys, all_vals = pl.pallas_call(
            functools.partial(score_kernel, planes, slots),
            out_shape=(shape((lax.axis_size("mp"), 1, DH), f32), together, together),
            in_specs=[smem] + [vmem] * 6,
            out_specs=(vmem, vmem, vmem),
            compiler_params=limit(16),
        )(meta, got, across, lastq, probes, own_s, own_p)
        parts = lax.all_to_all(score, "mp", 0, 0)
        attended = pl.pallas_call(
            functools.partial(attend_kernel, planes, slots),
            out_shape=shape(queries.shape, bf16),
            in_specs=[smem, smem] + [vmem] * 7,
            out_specs=vmem,
            scratch_shapes=[
                VMEM((slots, nheads, BLOCK, BLOCK), f32),
                VMEM((nheads, 8, BLOCK), f32),
                VMEM((nheads, 8, BLOCK), f32),
                VMEM((nheads, DH, BLOCK), f32),
            ],
            cost_estimate=pl.CostEstimate(flops=4 * 10**9, bytes_accessed=5 * 10**6, transcendentals=4 * 10**6),
            compiler_params=limit(10 + 2 * slots),
        )(step_lengths, meta, queries, all_keys, all_vals, down, top, total, acc)
        return attended, parts

    branches = [functools.partial(rest, s) for s in SIZES]
    attended, parts = lax.switch(choice[0], branches, held, meta)
    return attended, jnp.sum(parts[:, 0, :1], axis=0)


def solution(mesh):
    in_specs = (
        P(("leaf", "seq"), "mp"),
        P(("leaf", "seq"), "mp"),
        P(("leaf", "seq"), "mp"),
        P("leaf", None),
        P("leaf"),
        P("mp"),
    )
    out_specs = (P(("leaf", "seq"), "mp"), P(("leaf", "seq")))
    return jax.shard_map(
        functools.partial(on_device, 2), mesh=mesh, in_specs=in_specs, out_specs=out_specs, check_vma=False
    )
```

time: 75.1 us -> 67.6 us (0.900)
  the two profiles are of different devices: /device:TPU:1 before, /device:TPU:2 now
where the time goes in v2:
time: 67.6 us; the launch traced here: 67.1 us
  waiting for transfers between devices  29.8 us (44%)
  starting transfers between devices  20.8 us (31%)
  Pallas kernels  14.4 us (21%)
  between operations  1.35 us (2%)
    all_to_all x1, waiting for transfers between devices, rest(): got = lax.all_to_all(packed, 'seq', 0, 0)  19.7 us
    all_to_all x1, starting transfers between devices, rest(): got = lax.all_to_all(packed, 'seq', 0, 0)  10.4 us
    all_to_all x1, starting transfers between devices, on_device(): held = lax.all_to_all(send, 'seq', 0, 0, axis_index_groups=groups)  7.1 us
    all_to_all x1, waiting for transfers between devices, on_device(): held = lax.all_to_all(send, 'seq', 0, 0, axis_index_groups=groups)  6.82 us
    pallas_call x1, Pallas kernels, rest(): pl.pallas_call(functools.partial(own_kernel, planes, slots), out_shape=(p...  4.63 us
    all_to_all x1, starting transfers between devices, rest(): parts = lax.all_to_all(score, 'mp', 0, 0)  3.32 us
    all_to_all x1, waiting for transfers between devices, rest(): parts = lax.all_to_all(score, 'mp', 0, 0)  3.28 us
    pallas_call x1, Pallas kernels, rest(): pl.pallas_call(functools.partial(pack_kernel, planes, slots), out_shape=s...  2.42 us
  transfers between devices with their start and end apart: 3, of which 3 were waited for; matrix products, arithmetic and copies ran while one was open for 0% of the time, Pallas kernels for 13%

profile of v2, /device:TPU:2, one launch (start us, length us, event | category | flops | bytes accessed | tf_op | source)
XLA Modules:
  0.0 67.1 jit_solution(8008586449472795184)
XLA Ops:
  0.6 1.7 %shard_map.110 = bf16[8,64,128]{2,1,0:T(8,128)(2,1)} custom-call(s32[16,16]{1,0:T(8,128)} %mask_ref.3, s32[16]{0:T(128)} %len_ref.3, bf16[256,128]{1,0:T(8,128)(2,1)} %k_ref.1, bf16[256,128]{1,0:T(8,128)(2,1)} %v_ref.1), custom_call_target="tpu_custom_call" | custom-call | tf_op jit(solution)/shard_map/pallas_call | solution.py:257
  2.3 7.1 %all-to-all-start.16 = ((bf16[8,64,128]{2,1,0:T(8,128)(2,1)}), bf16[8,64,128]{2,1,0:T(8,128)(2,1)S(1)}, u32[]{:S(2)}, u32[]{:S(2)}) async-start(bf16[8,64,128]{2,1,0:T(8,128)(2,1)} %shard_map.110), calls=%async_computation.16 | async-start | bytes 262144 | tf_op jit(solution)/shard_map/all_to_all | solution.py:265
  9.4 1.6 %shard_map.109 = (s32[18]{0:T(128)S(1)}, s32[1]{0:T(128)}) custom-call(s32[16,16]{1,0:T(8,128)} %mask_ref.3, s32[16]{0:T(128)} %len_ref.3), custom_call_target="tpu_custom_call" | custom-call | flops 100000000 | bytes 100000 | tf_op jit(solution)/shard_map/pallas_call | solution.py:266
  11.7 6.8 %all-to-all-done.16 = bf16[8,64,128]{2,1,0:T(8,128)(2,1)S(1)} async-done(((bf16[8,64,128]{2,1,0:T(8,128)(2,1)}), bf16[8,64,128]{2,1,0:T(8,128)(2,1)S(1)}, u32[]{:S(2)}, u32[]{:S(2)}) %all-to-all-start.16) | async-done | bytes 131104 | tf_op jit(solution)/shard_map/all_to_all | solution.py:265
  18.5 48.5 %conditional.1 = (bf16[256,1024]{1,0:T(8,128)(2,1)}, f32[1]{0:T(128)}) conditional(s32[]{:T(128)} %bitcast.8, (s32[16,16]{1,0:T(8,128)}, s32[16]{0:T(128)}, s32[18]{0:T(128)S(1)}, bf16[8,64,128]{2,1,0:T(8,128)(2,1)S(1)}, bf16[1024]{0:T(1024)(128)(2,1)}, /*index=5*/bf16[256,1024]{1,0:T(8,128)(2,1)}, ...), branch_computations={%region_0.2_spmd, %region_2.4_spmd, %region_4.6_spmd, %region_6.8_... | conditional | flops 5000000000 | bytes 61409632 | solution.py:326
  18.5 0.0 copy-start.25
  18.5 0.0 copy-start.18
  18.5 0.0 copy-start.32
  18.5 0.0 copy-start.39
  18.5 0.0 copy-start.47
  18.5 0.0 copy-start.55
  18.6 2.4 %branch_2_fun.4 = bf16[16,160,128]{2,1,0:T(8,128)(2,1)} custom-call(s32[16,16]{1,0:T(8,128)} %get-tuple-element.172.mask_ref, s32[16]{0:T(128)} %get-tuple-element.169.len_ref, s32[18]{0:T(128)S(1)} %get-tuple-element.170.meta_ref, bf16[8,64,128]{2,1,0:T(8,128)(2,1)S(1)} %get-tuple-element.173.held_ref), custom_call_target="tpu_custom_call" | custom-call | tf_op jit(solution)/shard_map/cond/branch_2_fun/pallas_call | solution.py:276
  21.0 10.4 %all-to-all-start.4 = ((bf16[16,160,128]{2,1,0:T(8,128)(2,1)}), bf16[16,160,128]{2,1,0:T(8,128)(2,1)S(1)}, u32[]{:S(2)}, u32[]{:S(2)}) async-start(bf16[16,160,128]{2,1,0:T(8,128)(2,1)} %branch_2_fun.4), calls=%async_computation.4 | async-start | bytes 1310720 | tf_op jit(solution)/shard_map/cond/branch_2_fun/all_to_all | solution.py:284
  31.4 0.0 copy-done.25
  31.4 0.0 copy-done.18
  31.4 0.0 copy-done.32
  31.4 0.0 copy-done.39
  31.4 0.0 copy-done.47
  31.4 0.0 copy-done.55
  31.4 4.6 %branch_2_fun.5 = (f32[8,1,256]{2,1,0:T(1,128)S(1)}, f32[8,1,256]{2,1,0:T(1,128)S(1)}, f32[8,128,256]{2,1,0:T(8,128)S(1)}, f32[5,256]{1,0:T(8,128)S(1)}, f32[128...) custom-call(s32[16,16]{1,0:T(8,128)S(1)} %copy-done.18, ...), custom_call_target="tpu_custom_call" | custom-call | flops 1000000000 | bytes 5000000 | tf_op jit(solution)/shard_map/cond/branch_2_fun/pallas_call | solution.py:287
  36.1 19.7 %all-to-all-done.4.got_ref = bf16[16,160,128]{2,1,0:T(8,128)(2,1)S(1)} async-done(((bf16[16,160,128]{2,1,0:T(8,128)(2,1)}), bf16[16,160,128]{2,1,0:T(8,128)(2,1)S(1)}, u32[]{:S(2)}, u32[]{:S(2)}) %all-to-all-start.4) | async-done | bytes 655392 | tf_op jit(solution)/shard_map/cond/branch_2_fun/all_to_all | solution.py:284
  55.8 1.8 %branch_2_fun.6 = (f32[8,1,128]{2,1,0:T(1,128)}, bf16[1536,128]{1,0:T(8,128)(2,1)S(1)}, bf16[1536,128]{1,0:T(8,128)(2,1)S(1)}) custom-call(s32[18]{0:T(128)S(1)} %get-tuple-element.170.meta_ref, bf16[16,160,128]{2,1,0:T(8,128)(2,1)S(1)} %all-to-all-done.4.got_ref, f32[5,256]{1,0:T(8,128)S(1)} %get-tuple-element.177.across_ref, ...), custom_call_target="tpu_custom_call" | custom-call | tf_op jit(solution)/shard_map/cond/branch_2_fun/pallas_call | solution.py:301
  57.6 3.3 %all-to-all-start.5 = ((f32[8,1,128]{2,1,0:T(1,128)}), f32[8,1,128]{2,1,0:T(1,128)S(1)}, u32[]{:S(2)}, u32[]{:S(2)}) async-start(f32[8,1,128]{2,1,0:T(1,128)} %get-tuple-element.188), calls=%async_computation.5 | async-start | bytes 8192 | tf_op jit(solution)/shard_map/cond/branch_2_fun/all_to_all | solution.py:308
  61.0 2.2 %branch_2_fun.7 = bf16[256,1024]{1,0:T(8,128)(2,1)} custom-call(s32[16]{0:T(128)S(1)} %copy-done.47, s32[18]{0:T(128)S(1)} %get-tuple-element.170.meta_ref, bf16[256,1024]{1,0:T(8,128)(2,1)} %get-tuple-element.323.q_ref, bf16[1536,128]{1,0:T(8,128)(2,1)S(1)} %get-tuple-element.182.keys_ref, bf16[1536,128]{1,0:T(8,128)(2,1)S(1)} %get-tuple-element.183.vals_ref, ...), custom_call_target="tpu_custom_call" | custom-call | flops 4000000000 | bytes 5000000 | tf_op jit(solution)/shard_map/cond/branch_2_fun/pallas_call | solution.py:309
  63.2 3.3 %all-to-all-done.5 = f32[8,1,128]{2,1,0:T(1,128)S(1)} async-done(((f32[8,1,128]{2,1,0:T(1,128)}), f32[8,1,128]{2,1,0:T(1,128)S(1)}, u32[]{:S(2)}, u32[]{:S(2)}) %all-to-all-start.5) | async-done | bytes 4128 | tf_op jit(solution)/shard_map/cond/branch_2_fun/all_to_all | solution.py:308
  66.4 0.6 slice_reduce_fusion.2
  (1 shorter events, 0.0 us)
Async XLA Ops:
  2.3 16.2 %all-to-all-start.16 = ((bf16[8,64,128]{2,1,0:T(8,128)(2,1)}), bf16[8,64,128]{2,1,0:T(8,128)(2,1)S(1)}, u32[]{:S(2)}, u32[]{:S(2)}) async-start(bf16[8,64,128]{2,1,0:T(8,128)(2,1)} %shard_map.110), calls=%async_computation.16 | async-start | bytes 262144 | tf_op jit(solution)/shard_map/all_to_all | solution.py:265
  18.5 12.9 %copy-start.25 = (bf16[1024]{0:T(1024)(128)(2,1)S(1)}, bf16[1024]{0:T(1024)(128)(2,1)}, u32[]{:S(2)}) copy-start(bf16[1024]{0:T(1024)(128)(2,1)} %get-tuple-element.315) | copy-start | bytes 6148 | tf_op jit(solution)/shard_map/cond
  18.5 12.9 %copy-start.18 = (s32[16,16]{1,0:T(8,128)S(1)}, s32[16,16]{1,0:T(8,128)}, u32[]{:S(2)}) copy-start(s32[16,16]{1,0:T(8,128)} %get-tuple-element.172.mask_ref) | copy-start | bytes 3076 | tf_op jit(solution)/shard_map/cond
  18.5 12.9 %copy-start.32 = (bf16[256,128]{1,0:T(8,128)(2,1)S(1)}, bf16[256,128]{1,0:T(8,128)(2,1)}, u32[]{:S(2)}) copy-start(bf16[256,128]{1,0:T(8,128)(2,1)} %get-tuple-element.174.k_ref) | copy-start | bytes 196612 | tf_op jit(solution)/shard_map/cond
  18.5 12.9 %copy-start.39 = (bf16[256,128]{1,0:T(8,128)(2,1)S(1)}, bf16[256,128]{1,0:T(8,128)(2,1)}, u32[]{:S(2)}) copy-start(bf16[256,128]{1,0:T(8,128)(2,1)} %get-tuple-element.175.v_ref) | copy-start | bytes 196612 | tf_op jit(solution)/shard_map/cond
  18.5 12.9 %copy-start.47 = (s32[16]{0:T(128)S(1)}, s32[16]{0:T(128)}, u32[]{:S(2)}) copy-start(s32[16]{0:T(128)} %get-tuple-element.169.len_ref) | copy-start | bytes 196 | tf_op jit(solution)/shard_map/cond
  18.5 12.9 %copy-start.55 = (bf16[256,1024]{1,0:T(8,128)(2,1)S(1)}, bf16[256,1024]{1,0:T(8,128)(2,1)}, u32[]{:S(2)}) copy-start(bf16[256,1024]{1,0:T(8,128)(2,1)} %get-tuple-element.323.q_ref) | copy-start | bytes 1572868 | tf_op jit(solution)/shard_map/cond
  21.0 34.8 %all-to-all-start.4 = ((bf16[16,160,128]{2,1,0:T(8,128)(2,1)}), bf16[16,160,128]{2,1,0:T(8,128)(2,1)S(1)}, u32[]{:S(2)}, u32[]{:S(2)}) async-start(bf16[16,160,128]{2,1,0:T(8,128)(2,1)} %branch_2_fun.4), calls=%async_computation.4 | async-start | bytes 1310720 | tf_op jit(solution)/shard_map/cond/branch_2_fun/all_to_all | solution.py:284
  57.6 8.8 %all-to-all-start.5 = ((f32[8,1,128]{2,1,0:T(1,128)}), f32[8,1,128]{2,1,0:T(1,128)S(1)}, u32[]{:S(2)}, u32[]{:S(2)}) async-start(f32[8,1,128]{2,1,0:T(1,128)} %get-tuple-element.188), calls=%async_computation.5 | async-start | bytes 8192 | tf_op jit(solution)/shard_map/cond/branch_2_fun/all_to_all | solution.py:308

commit v3 on v2

--- a/solution.py
+++ b/solution.py
@@ -81,14 +81,17 @@
         for k in range(PER_KEYS // holders):
             chunk = first + k * holders
             slot = jnp.minimum((start + chunk) // holders, slots - 1)
-            row = pl.multiple_of(slot * PAIR, PAIR)
+            row = pl.multiple_of(slot * CHUNK, CHUNK)
             used = jnp.where(chunk < count, 1, 0)
-            piece = held_ref[y, k * PAIR : (k + 1) * PAIR, :]
+            key = held_ref[y, k * PAIR : k * PAIR + CHUNK, :]
+            value = held_ref[y, k * PAIR + CHUNK : (k + 1) * PAIR, :]
             for j in range(y * planes + 1, nblocks):
                 needed = mask_ref[j, block] * used
                 if j < (y + 1) * planes:
                     needed = jnp.where(block < j, needed, 0)
-                work[jnp.where(needed > 0, j, nblocks), pl.ds(row, PAIR), :] = piece
+                to = jnp.where(needed > 0, j, nblocks)
+                work[to, pl.ds(row, CHUNK), :] = key
+                work[to, pl.ds(slots * CHUNK + row, CHUNK), :] = value
     send_ref[...] = work[:nblocks]
 
 
@@ -101,18 +104,22 @@
     length = len_ref[me]
     nheads = q_ref.shape[1] // DH
     scale = 1.0 / math.sqrt(DH)
-    row_at = lax.broadcasted_iota(jnp.int32, (slots, BLOCK), 0) * BLOCK
-    row_at = row_at + lax.broadcasted_iota(jnp.int32, (slots, BLOCK), 1)
+    holders = nblocks // planes
+    lane = lax.broadcasted_iota(jnp.int32, (1, slots * BLOCK), 1)
+    source = ((lane.astype(jnp.float32) + 0.5) * (1.0 / (slots * CHUNK))).astype(jnp.int32)
+    within = lane - source * (slots * CHUNK)
+    row_at = (within // CHUNK * holders + source // planes) * CHUNK + within % CHUNK
+    of_plane = source % planes
     row_id = lax.broadcasted_iota(jnp.int32, (CHUNK, DH), 0)
-    allowed = jnp.zeros((slots, BLOCK), jnp.int32)
+    allowed = jnp.zeros(lane.shape, jnp.int32)
     down_ref[...] = jnp.full(down_ref.shape, NEG, jnp.float32)
     for b in range(nblocks - 1):
         before = meta_ref[b]
         for plane in range(b % planes):
             before += meta_ref[nblocks + plane]
         used = jnp.where((mask_ref[me, b] > 0) & (b < me), len_ref[b], 0)
-        row = row_at - before * CHUNK
-        allowed = jnp.where((row >= 0) & (row < used), 1, allowed)
+        row = row_at - meta_ref[b] * CHUNK
+        allowed = jnp.where((of_plane == b % planes) & (row >= 0) & (row < used), 1, allowed)
 
         def one_chunk(c, carry):
             at = pl.multiple_of((before + c) * CHUNK, CHUNK)
@@ -154,56 +161,47 @@
     own_p_ref[...] = lax.dot_general(probes, v_ref[...], NT, preferred_element_type=jnp.float32)
 
 
-def score_kernel(
-    planes, slots, meta_ref, got_ref, across_ref, lastq_ref, probes_ref, own_s_ref, own_p_ref, score_ref, keys_ref, vals_ref,
-):
+def score_kernel(slots, got_ref, across_ref, lastq_ref, probes_ref, own_s_ref, own_p_ref, score_ref):
     nblocks = got_ref.shape[0]
-    holders = nblocks // planes
     scale = 1.0 / math.sqrt(DH)
-    zeros = jnp.zeros((BLOCK, DH), jnp.bfloat16)
-    before = jnp.int32(0)
-    for plane in range(planes):
-        tail = pl.multiple_of((before + slots * holders) * CHUNK, CHUNK)
-        if plane == 0:
-            keys_ref[slots * holders * CHUNK :, :] = jnp.zeros_like(keys_ref[slots * holders * CHUNK :, :])
-            vals_ref[slots * holders * CHUNK :, :] = jnp.zeros_like(vals_ref[slots * holders * CHUNK :, :])
-        else:
-            keys_ref[pl.ds(tail, BLOCK), :] = zeros
-            vals_ref[pl.ds(tail, BLOCK), :] = zeros
-        for s in range(slots):
-            for p in range(holders):
-                at = pl.multiple_of((before + s * holders + p) * CHUNK, CHUNK)
-                i = p * planes + plane
-                keys_ref[pl.ds(at, CHUNK), :] = got_ref[i, s * PAIR : s * PAIR + CHUNK, :]
-                vals_ref[pl.ds(at, CHUNK), :] = got_ref[i, s * PAIR + CHUNK : (s + 1) * PAIR, :]
-        before += meta_ref[nblocks + plane]
+    half = slots * CHUNK
     lastq = lastq_ref[...].astype(jnp.bfloat16)
     probes = probes_ref[...].astype(jnp.bfloat16)
-    scores, products = [own_s_ref[...]], [own_p_ref[...]]
-    for s in range(slots):
-        rows = slice(s * BLOCK, (s + 1) * BLOCK)
-        part = lax.dot_general(lastq, keys_ref[rows, :], NT, preferred_element_type=jnp.float32)
-        scores.append(part + across_ref[s : s + 1, :])
-        products.append(
-            lax.dot_general(probes, vals_ref[rows, :], NT, preferred_element_type=jnp.float32)
-        )
-    top = jnp.max(functools.reduce(jnp.maximum, scores), axis=1, keepdims=True)
-    weights = [jnp.exp((part - top) * scale) for part in scores]
-    total = jnp.sum(sum(weights), axis=1, keepdims=True)
-    mixed = jnp.sum(sum(w * p for w, p in zip(weights, products)), axis=1, keepdims=True)
+    keys = jnp.concatenate([got_ref[i, :half, :] for i in range(nblocks)], axis=0)
+    vals = jnp.concatenate([got_ref[i, half:, :] for i in range(nblocks)], axis=0)
+    scores = lax.dot_general(lastq, keys, NT, preferred_element_type=jnp.float32) + across_ref[...]
+    products = lax.dot_general(probes, vals, NT, preferred_element_type=jnp.float32)
+    own_s = own_s_ref[...]
+    top = jnp.maximum(jnp.max(scores, axis=1, keepdims=True), jnp.max(own_s, axis=1, keepdims=True))
+    w = jnp.exp((scores - top) * scale)
+    own_w = jnp.exp((own_s - top) * scale)
+    total = jnp.sum(w, axis=1, keepdims=True) + jnp.sum(own_w, axis=1, keepdims=True)
+    mixed = jnp.sum(w * products, axis=1, keepdims=True) + jnp.sum(own_w * own_p_ref[...], axis=1, keepdims=True)
     score_ref[...] = jnp.full(score_ref.shape, jnp.sum(mixed / total), jnp.float32)
 
 
 def attend_kernel(
-    planes, slots, len_ref, meta_ref, q_ref, keys_ref, vals_ref, down_ref, top_ref, total_ref, acc_ref, out_ref,
-    kept, tops, totals, accs,
+    planes, slots, len_ref, meta_ref, q_ref, got_ref, down_ref, top_ref, total_ref, acc_ref, out_ref,
+    keys, vals, kept, tops, totals, accs,
 ):
     length = len_ref[lax.axis_index("seq")]
     nblocks = len_ref.shape[0]
     nheads = q_ref.shape[1] // DH
     scale = 1.0 / math.sqrt(DH)
+    holders = nblocks // planes
+    half = slots * CHUNK
     count = jnp.int32(0)
     for plane in range(planes):
+        for s in range(slots):
+            for p in range(holders):
+                at = pl.multiple_of((count + s * holders + p) * CHUNK, CHUNK)
+                i = p * planes + plane
+                keys[pl.ds(at, CHUNK), :] = got_ref[i, s * CHUNK : (s + 1) * CHUNK, :]
+                vals[pl.ds(at, CHUNK), :] = got_ref[i, half + s * CHUNK : half + (s + 1) * CHUNK, :]
+        if plane == planes - 1:
+            tail = pl.multiple_of((count + slots * holders) * CHUNK, CHUNK)
+            keys[pl.ds(tail, BLOCK), :] = jnp.zeros((BLOCK, DH), jnp.bfloat16)
+            vals[pl.ds(tail, BLOCK), :] = jnp.zeros((BLOCK, DH), jnp.bfloat16)
         count += meta_ref[nblocks + plane]
     steps = (count + PER_KEYS - 1) // PER_KEYS
     for h in range(nheads):
@@ -215,7 +213,7 @@
         bias = jnp.concatenate([bias, bias], axis=1)
         for h in range(nheads):
             q = q_ref[:, h * DH : (h + 1) * DH]
-            part = lax.dot_general(keys_ref[at, :], q, NT, preferred_element_type=jnp.float32) + bias
+            part = lax.dot_general(keys[at, :], q, NT, preferred_element_type=jnp.float32) + bias
             kept[n, h] = part
             tops[h] = jnp.maximum(tops[h], jnp.max(part.reshape(BLOCK // 8, 8, BLOCK), axis=0))
         return carry
@@ -231,7 +229,7 @@
 
     def one_mix(n, carry):
         at = pl.ds(pl.multiple_of(n * BLOCK, BLOCK), BLOCK)
-        vt = jnp.transpose(vals_ref[at, :].astype(jnp.float32)).astype(jnp.bfloat16)
+        vt = jnp.transpose(vals[at, :].astype(jnp.float32)).astype(jnp.bfloat16)
         for h in range(nheads):
             w = jnp.exp((kept[n, h] - tops[h, :1, :]) * scale)
             totals[h] += jnp.sum(w.reshape(BLOCK // 8, 8, BLOCK), axis=0)
@@ -287,7 +285,7 @@
         top, total, acc, across, down, lastq, probes, own_s, own_p = pl.pallas_call(
             functools.partial(own_kernel, planes, slots),
             out_shape=(
-                per_head, per_head, shape((nheads, DH, BLOCK), f32), shape((slots, BLOCK), f32),
+                per_head, per_head, shape((nheads, DH, BLOCK), f32), shape((1, slots * BLOCK), f32),
                 shape((slots * BLOCK, DH), f32), small, small,
                 shape((nheads, BLOCK), f32), shape((nheads, BLOCK), f32),
             ),
@@ -297,21 +295,22 @@
             cost_estimate=pl.CostEstimate(flops=10**9, bytes_accessed=5 * 10**6, transcendentals=10**6),
             compiler_params=limit(12),
         )(tree_mask, step_lengths, meta, queries, keys, values, probe.reshape(1, -1))
-        together = shape((slots * BLOCK + BLOCK, DH), bf16)
-        score, all_keys, all_vals = pl.pallas_call(
-            functools.partial(score_kernel, planes, slots),
-            out_shape=(shape((lax.axis_size("mp"), 1, DH), f32), together, together),
-            in_specs=[smem] + [vmem] * 6,
-            out_specs=(vmem, vmem, vmem),
+        score = pl.pallas_call(
+            functools.partial(score_kernel, slots),
+            out_shape=shape((lax.axis_size("mp"), 1, DH), f32),
+            in_specs=[vmem] * 6,
+            out_specs=vmem,
             compiler_params=limit(16),
-        )(meta, got, across, lastq, probes, own_s, own_p)
+        )(got, across, lastq, probes, own_s, own_p)
         parts = lax.all_to_all(score, "mp", 0, 0)
         attended = pl.pallas_call(
             functools.partial(attend_kernel, planes, slots),
             out_shape=shape(queries.shape, bf16),
-            in_specs=[smem, smem] + [vmem] * 7,
+            in_specs=[smem, smem] + [vmem] * 6,
             out_specs=vmem,
             scratch_shapes=[
+                VMEM((slots * BLOCK + BLOCK, DH), bf16),
+                VMEM((slots * BLOCK + BLOCK, DH), bf16),
                 VMEM((slots, nheads, BLOCK, BLOCK), f32),
                 VMEM((nheads, 8, BLOCK), f32),
                 VMEM((nheads, 8, BLOCK), f32),
@@ -319,7 +318,7 @@
             ],
             cost_estimate=pl.CostEstimate(flops=4 * 10**9, bytes_accessed=5 * 10**6, transcendentals=4 * 10**6),
             compiler_params=limit(10 + 2 * slots),
-        )(step_lengths, meta, queries, all_keys, all_vals, down, top, total, acc)
+        )(step_lengths, meta, queries, got, down, top, total, acc)
         return attended, parts
 
     branches = [functools.partial(rest, s) for s in SIZES]

time: 67.6 us -> 73 us (1.080)
  the two profiles are of different devices: /device:TPU:2 before, /device:TPU:59 now
where the time goes in v3:
time: 73 us; the launch traced here: 72.4 us
  starting transfers between devices  28.7 us (39%)
  waiting for transfers between devices  22.1 us (30%)
  Pallas kernels  19.4 us (27%)
  between operations  1.44 us (2%)
    all_to_all x1, waiting for transfers between devices, rest(): got = lax.all_to_all(packed, 'seq', 0, 0)  19.6 us
    all_to_all x1, starting transfers between devices, rest(): got = lax.all_to_all(packed, 'seq', 0, 0)  13.7 us
    all_to_all x1, starting transfers between devices, rest(): parts = lax.all_to_all(score, 'mp', 0, 0)  8.75 us
    pallas_call x1, Pallas kernels, rest(): pl.pallas_call(functools.partial(attend_kernel, planes, slots), out_shape...  7.21 us
    all_to_all x1, starting transfers between devices, on_device(): held = lax.all_to_all(send, 'seq', 0, 0, axis_index_groups=groups)  6.31 us
    pallas_call x1, Pallas kernels, rest(): pl.pallas_call(functools.partial(own_kernel, planes, slots), out_shape=(p...  5.15 us
    pallas_call x1, Pallas kernels, rest(): pl.pallas_call(functools.partial(pack_kernel, planes, slots), out_shape=s...  2.61 us
    all_to_all x1, waiting for transfers between devices, on_device(): held = lax.all_to_all(send, 'seq', 0, 0, axis_index_groups=groups)  2.58 us
  transfers between devices with their start and end apart: 3, of which 2 were waited for; matrix products, arithmetic and copies ran while one was open for 0% of the time, Pallas kernels for 19%

profile of v3, /device:TPU:59, one launch (start us, length us, event | category | flops | bytes accessed | tf_op | source)
XLA Modules:
  0.0 72.4 jit_solution(3830987353068829382)
XLA Ops:
  0.6 1.7 %shard_map.110 = bf16[8,64,128]{2,1,0:T(8,128)(2,1)} custom-call(s32[16,16]{1,0:T(8,128)} %mask_ref.3, s32[16]{0:T(128)} %len_ref.3, bf16[256,128]{1,0:T(8,128)(2,1)} %k_ref.1, bf16[256,128]{1,0:T(8,128)(2,1)} %v_ref.1), custom_call_target="tpu_custom_call" | custom-call | tf_op jit(solution)/shard_map/pallas_call | solution.py:255
  2.3 6.3 %all-to-all-start.16 = ((bf16[8,64,128]{2,1,0:T(8,128)(2,1)}), bf16[8,64,128]{2,1,0:T(8,128)(2,1)S(1)}, u32[]{:S(2)}, u32[]{:S(2)}) async-start(bf16[8,64,128]{2,1,0:T(8,128)(2,1)} %shard_map.110), calls=%async_computation.16 | async-start | bytes 262144 | tf_op jit(solution)/shard_map/all_to_all | solution.py:263
  8.6 1.6 %shard_map.109 = (s32[18]{0:T(128)S(1)}, s32[1]{0:T(128)}) custom-call(s32[16,16]{1,0:T(8,128)} %mask_ref.3, s32[16]{0:T(128)} %len_ref.3), custom_call_target="tpu_custom_call" | custom-call | flops 100000000 | bytes 100000 | tf_op jit(solution)/shard_map/pallas_call | solution.py:264
  10.9 2.6 %all-to-all-done.16 = bf16[8,64,128]{2,1,0:T(8,128)(2,1)S(1)} async-done(((bf16[8,64,128]{2,1,0:T(8,128)(2,1)}), bf16[8,64,128]{2,1,0:T(8,128)(2,1)S(1)}, u32[]{:S(2)}, u32[]{:S(2)}) %all-to-all-start.16) | async-done | bytes 131104 | tf_op jit(solution)/shard_map/all_to_all | solution.py:263
  13.5 58.8 %conditional.1 = (bf16[256,1024]{1,0:T(8,128)(2,1)}, f32[1]{0:T(128)}) conditional(s32[]{:T(128)} %bitcast.8, (s32[16,16]{1,0:T(8,128)}, s32[16]{0:T(128)}, s32[18]{0:T(128)S(1)}, bf16[8,64,128]{2,1,0:T(8,128)(2,1)S(1)}, bf16[1024]{0:T(1024)(128)(2,1)}, /*index=5*/bf16[256,1024]{1,0:T(8,128)(2,1)}, ...), branch_computations={%region_0.2_spmd, %region_2.4_spmd, %region_4.6_spmd, %region_6.8_... | conditional | flops 5000000000 | bytes 42010836 | solution.py:325
  13.5 0.0 copy-start.12
  13.5 0.0 copy-start.6
  13.5 0.0 copy-start.18
  13.5 0.0 copy-start.24
  13.5 0.0 copy-start.32
  13.5 0.0 copy-start.40
  13.5 2.6 %branch_3_fun.4 = bf16[16,192,128]{2,1,0:T(8,128)(2,1)} custom-call(s32[16,16]{1,0:T(8,128)} %get-tuple-element.183.mask_ref, s32[16]{0:T(128)} %get-tuple-element.180.len_ref, s32[18]{0:T(128)S(1)} %get-tuple-element.181.meta_ref, bf16[8,64,128]{2,1,0:T(8,128)(2,1)S(1)} %get-tuple-element.184.held_ref), custom_call_target="tpu_custom_call" | custom-call | tf_op jit(solution)/shard_map/cond/branch_3_fun/pallas_call | solution.py:274
  16.1 13.7 %all-to-all-start.6 = ((bf16[16,192,128]{2,1,0:T(8,128)(2,1)}), bf16[16,192,128]{2,1,0:T(8,128)(2,1)S(1)}, u32[]{:S(2)}, u32[]{:S(2)}) async-start(bf16[16,192,128]{2,1,0:T(8,128)(2,1)} %branch_3_fun.4), calls=%async_computation.6 | async-start | bytes 1572864 | tf_op jit(solution)/shard_map/cond/branch_3_fun/all_to_all | solution.py:282
  29.8 0.0 copy-done.12
  29.8 0.0 copy-done.6
  29.8 0.0 copy-done.18
  29.9 0.0 copy-done.24
  29.9 0.0 copy-done.32
  29.9 0.0 copy-done.40
  29.9 5.1 %branch_3_fun.5 = (f32[8,1,256]{2,1,0:T(1,128)S(1)}, f32[8,1,256]{2,1,0:T(1,128)S(1)}, f32[8,128,256]{2,1,0:T(8,128)S(1)}, f32[1,1536]{1,0:T(1,128)S(1)}, f32[15...) custom-call(s32[16,16]{1,0:T(8,128)S(1)} %copy-done.6, ...), custom_call_target="tpu_custom_call" | custom-call | flops 1000000000 | bytes 5000000 | tf_op jit(solution)/shard_map/cond/branch_3_fun/pallas_call | solution.py:285
  35.0 19.6 %all-to-all-done.6.got_ref = bf16[16,192,128]{2,1,0:T(8,128)(2,1)S(1)} async-done(((bf16[16,192,128]{2,1,0:T(8,128)(2,1)}), bf16[16,192,128]{2,1,0:T(8,128)(2,1)S(1)}, u32[]{:S(2)}, u32[]{:S(2)}) %all-to-all-start.6) | async-done | bytes 786464 | tf_op jit(solution)/shard_map/cond/branch_3_fun/all_to_all | solution.py:282
  54.6 1.1 %branch_3_fun.7 = f32[8,1,128]{2,1,0:T(1,128)} custom-call(bf16[16,192,128]{2,1,0:T(8,128)(2,1)S(1)} %all-to-all-done.6.got_ref, f32[1,1536]{1,0:T(1,128)S(1)} %get-tuple-element.192.across_ref, f32[8,128]{1,0:T(8,128)S(1)} %get-tuple-element.193.lastq_ref, f32[8,128]{1,0:T(8,128)S(1)} %get-tuple-element.194.probes_ref, ...), custom_call_target="tpu_custom_call" | custom-call | tf_op jit(solution)/shard_map/cond/branch_3_fun/pallas_call | solution.py:298
  55.7 8.7 %all-to-all-start.7 = ((f32[8,1,128]{2,1,0:T(1,128)}), f32[8,1,128]{2,1,0:T(1,128)S(1)}, u32[]{:S(2)}, u32[]{:S(2)}) async-start(f32[8,1,128]{2,1,0:T(1,128)} %branch_3_fun.7), calls=%async_computation.7 | async-start | bytes 8192 | tf_op jit(solution)/shard_map/cond/branch_3_fun/all_to_all | solution.py:305
  64.5 7.2 %branch_3_fun.6 = bf16[256,1024]{1,0:T(8,128)(2,1)} custom-call(s32[16]{0:T(128)S(1)} %copy-done.32, s32[18]{0:T(128)S(1)} %get-tuple-element.181.meta_ref, bf16[256,1024]{1,0:T(8,128)(2,1)S(1)} %copy-done.40, bf16[16,192,128]{2,1,0:T(8,128)(2,1)S(1)} %all-to-all-done.6.got_ref, f32[1536,128]{1,0:T(8,128)S(1)} %get-tuple-element.188.down_ref, ...), custom_call_target="tpu_custom_call" | custom-call | flops 4000000000 | bytes 5000000 | tf_op jit(solution)/shard_map/cond/branch_3_fun/pallas_call | solution.py:306
  71.7 0.0 all-to-all-done.7
  71.7 0.6 slice_reduce_fusion.3
  (1 shorter events, 0.0 us)
Async XLA Ops:
  2.3 11.2 %all-to-all-start.16 = ((bf16[8,64,128]{2,1,0:T(8,128)(2,1)}), bf16[8,64,128]{2,1,0:T(8,128)(2,1)S(1)}, u32[]{:S(2)}, u32[]{:S(2)}) async-start(bf16[8,64,128]{2,1,0:T(8,128)(2,1)} %shard_map.110), calls=%async_computation.16 | async-start | bytes 262144 | tf_op jit(solution)/shard_map/all_to_all | solution.py:263
  13.5 16.3 %copy-start.12 = (bf16[1024]{0:T(1024)(128)(2,1)S(1)}, bf16[1024]{0:T(1024)(128)(2,1)}, u32[]{:S(2)}) copy-start(bf16[1024]{0:T(1024)(128)(2,1)} %get-tuple-element.292) | copy-start | bytes 6148 | tf_op jit(solution)/shard_map/cond
  13.5 16.4 %copy-start.6 = (s32[16,16]{1,0:T(8,128)S(1)}, s32[16,16]{1,0:T(8,128)}, u32[]{:S(2)}) copy-start(s32[16,16]{1,0:T(8,128)} %get-tuple-element.183.mask_ref) | copy-start | bytes 3076 | tf_op jit(solution)/shard_map/cond
  13.5 16.4 %copy-start.18 = (bf16[256,128]{1,0:T(8,128)(2,1)S(1)}, bf16[256,128]{1,0:T(8,128)(2,1)}, u32[]{:S(2)}) copy-start(bf16[256,128]{1,0:T(8,128)(2,1)} %get-tuple-element.185.k_ref) | copy-start | bytes 196612 | tf_op jit(solution)/shard_map/cond
  13.5 16.4 %copy-start.24 = (bf16[256,128]{1,0:T(8,128)(2,1)S(1)}, bf16[256,128]{1,0:T(8,128)(2,1)}, u32[]{:S(2)}) copy-start(bf16[256,128]{1,0:T(8,128)(2,1)} %get-tuple-element.186.v_ref) | copy-start | bytes 196612 | tf_op jit(solution)/shard_map/cond
  13.5 16.4 %copy-start.32 = (s32[16]{0:T(128)S(1)}, s32[16]{0:T(128)}, u32[]{:S(2)}) copy-start(s32[16]{0:T(128)} %get-tuple-element.180.len_ref) | copy-start | bytes 196 | tf_op jit(solution)/shard_map/cond
  13.5 16.4 %copy-start.40 = (bf16[256,1024]{1,0:T(8,128)(2,1)S(1)}, bf16[256,1024]{1,0:T(8,128)(2,1)}, u32[]{:S(2)}) copy-start(bf16[256,1024]{1,0:T(8,128)(2,1)} %get-tuple-element.300.q_ref) | copy-start | bytes 1572868 | tf_op jit(solution)/shard_map/cond
  16.1 38.5 %all-to-all-start.6 = ((bf16[16,192,128]{2,1,0:T(8,128)(2,1)}), bf16[16,192,128]{2,1,0:T(8,128)(2,1)S(1)}, u32[]{:S(2)}, u32[]{:S(2)}) async-start(bf16[16,192,128]{2,1,0:T(8,128)(2,1)} %branch_3_fun.4), calls=%async_computation.6 | async-start | bytes 1572864 | tf_op jit(solution)/shard_map/cond/branch_3_fun/all_to_all | solution.py:282
  55.7 16.0 %all-to-all-start.7 = ((f32[8,1,128]{2,1,0:T(1,128)}), f32[8,1,128]{2,1,0:T(1,128)S(1)}, u32[]{:S(2)}, u32[]{:S(2)}) async-start(f32[8,1,128]{2,1,0:T(1,128)} %branch_3_fun.7), calls=%async_computation.7 | async-start | bytes 8192 | tf_op jit(solution)/shard_map/cond/branch_3_fun/all_to_all | solution.py:305

commit v4 on v3

--- a/solution.py
+++ b/solution.py
@@ -25,14 +25,20 @@
     return (length + CHUNK - 1) // CHUNK
 
 
+def entry(row_ref, index):
+    row = row_ref[...].reshape(1, -1)
+    at = lax.broadcasted_iota(jnp.int32, row.shape, 1) == index
+    return jnp.sum(jnp.where(at, row, 0))
+
+
 def spread_kernel(planes, mask_ref, len_ref, k_ref, v_ref, send_ref):
     nblocks = mask_ref.shape[0]
     holders = nblocks // planes
     me = lax.axis_index("seq")
-    start = jnp.int32(0)
-    for a in range(nblocks - 1):
-        counted = (a < me) & (lax.rem(me, planes) == a % planes)
-        start += jnp.where(counted, mask_ref[me, a] * chunks_of(len_ref[a]), 0)
+    row = lax.broadcasted_iota(jnp.int32, mask_ref.shape, 0)
+    column = lax.broadcasted_iota(jnp.int32, mask_ref.shape, 1)
+    counted = (row == me) & (column < me) & (column % planes == lax.rem(me, planes))
+    start = jnp.sum(jnp.where(counted, mask_ref[...] * chunks_of(len_ref[...].reshape(1, -1)), 0))
     for chunk in range(PER_KEYS):
         holder = lax.rem(start + chunk, holders)
         row = (chunk // holders) * PAIR
@@ -184,7 +190,7 @@
     planes, slots, len_ref, meta_ref, q_ref, got_ref, down_ref, top_ref, total_ref, acc_ref, out_ref,
     keys, vals, kept, tops, totals, accs,
 ):
-    length = len_ref[lax.axis_index("seq")]
+    length = entry(len_ref, lax.axis_index("seq"))
     nblocks = len_ref.shape[0]
     nheads = q_ref.shape[1] // DH
     scale = 1.0 / math.sqrt(DH)
@@ -202,7 +208,7 @@
             tail = pl.multiple_of((count + slots * holders) * CHUNK, CHUNK)
             keys[pl.ds(tail, BLOCK), :] = jnp.zeros((BLOCK, DH), jnp.bfloat16)
             vals[pl.ds(tail, BLOCK), :] = jnp.zeros((BLOCK, DH), jnp.bfloat16)
-        count += meta_ref[nblocks + plane]
+        count += entry(meta_ref, nblocks + plane)
     steps = (count + PER_KEYS - 1) // PER_KEYS
     for h in range(nheads):
         tops[h] = jnp.broadcast_to(top_ref[h], (8, BLOCK))
@@ -255,7 +261,7 @@
     send = pl.pallas_call(
         functools.partial(spread_kernel, planes),
         out_shape=shape((holders, PER_KEYS // holders * PAIR, DH), bf16),
-        in_specs=[smem, smem, vmem, vmem],
+        in_specs=[vmem] * 4,
         out_specs=vmem,
         compiler_params=limit(8),
     )(tree_mask, step_lengths, keys, values)
@@ -306,7 +312,7 @@
         attended = pl.pallas_call(
             functools.partial(attend_kernel, planes, slots),
             out_shape=shape(queries.shape, bf16),
-            in_specs=[smem, smem] + [vmem] * 6,
+            in_specs=[vmem] * 8,
             out_specs=vmem,
             scratch_shapes=[
                 VMEM((slots * BLOCK + BLOCK, DH), bf16),

time: 73 us -> 69.4 us (0.951)
  the two profiles are of different devices: /device:TPU:59 before, /device:TPU:6 now
where the time goes in v4:
time: 69.4 us; the launch traced here: 70.3 us
  waiting for transfers between devices  34.2 us (49%)
  starting transfers between devices  20.8 us (30%)
  Pallas kernels  13.2 us (19%)
  between operations  1.44 us (2%)
    all_to_all x1, waiting for transfers between devices, rest(): got = lax.all_to_all(packed, 'seq', 0, 0)  23.2 us
    all_to_all x1, starting transfers between devices, rest(): got = lax.all_to_all(packed, 'seq', 0, 0)  10.4 us
    all_to_all x1, starting transfers between devices, on_device(): held = lax.all_to_all(send, 'seq', 0, 0, axis_index_groups=groups)  7.1 us
    all_to_all x1, waiting for transfers between devices, on_device(): held = lax.all_to_all(send, 'seq', 0, 0, axis_index_groups=groups)  6.82 us
    pallas_call x1, Pallas kernels, rest(): pl.pallas_call(functools.partial(own_kernel, planes, slots), out_shape=(p...  4.74 us
    all_to_all x1, waiting for transfers between devices, rest(): parts = lax.all_to_all(score, 'mp', 0, 0)  4.22 us
    all_to_all x1, starting transfers between devices, rest(): parts = lax.all_to_all(score, 'mp', 0, 0)  3.28 us
    pallas_call x1, Pallas kernels, rest(): pl.pallas_call(functools.partial(pack_kernel, planes, slots), out_shape=s...  2.61 us
  transfers between devices with their start and end apart: 3, of which 3 were waited for; matrix products, arithmetic and copies ran while one was open for 0% of the time, Pallas kernels for 11%

profile of v4, /device:TPU:6, one launch (start us, length us, event | category | flops | bytes accessed | tf_op | source)
XLA Modules:
  0.0 70.3 jit_solution(4735935200092398086)
XLA Ops:
  0.6 1.7 %shard_map.110 = bf16[8,64,128]{2,1,0:T(8,128)(2,1)} custom-call(s32[16,16]{1,0:T(8,128)} %mask_ref.3, s32[16]{0:T(128)} %len_ref.3, bf16[256,128]{1,0:T(8,128)(2,1)} %k_ref.1, bf16[256,128]{1,0:T(8,128)(2,1)} %v_ref.1), custom_call_target="tpu_custom_call" | custom-call | tf_op jit(solution)/shard_map/pallas_call | solution.py:261
  2.4 7.1 %all-to-all-start.16 = ((bf16[8,64,128]{2,1,0:T(8,128)(2,1)}), bf16[8,64,128]{2,1,0:T(8,128)(2,1)S(1)}, u32[]{:S(2)}, u32[]{:S(2)}) async-start(bf16[8,64,128]{2,1,0:T(8,128)(2,1)} %shard_map.110), calls=%async_computation.16 | async-start | bytes 262144 | tf_op jit(solution)/shard_map/all_to_all | solution.py:269
  9.5 1.6 %shard_map.109 = (s32[18]{0:T(128)S(1)}, s32[1]{0:T(128)}) custom-call(s32[16,16]{1,0:T(8,128)} %mask_ref.3, s32[16]{0:T(128)} %len_ref.3), custom_call_target="tpu_custom_call" | custom-call | flops 100000000 | bytes 100000 | tf_op jit(solution)/shard_map/pallas_call | solution.py:270
  11.7 6.8 %all-to-all-done.16 = bf16[8,64,128]{2,1,0:T(8,128)(2,1)S(1)} async-done(((bf16[8,64,128]{2,1,0:T(8,128)(2,1)}), bf16[8,64,128]{2,1,0:T(8,128)(2,1)S(1)}, u32[]{:S(2)}, u32[]{:S(2)}) %all-to-all-start.16) | async-done | bytes 131104 | tf_op jit(solution)/shard_map/all_to_all | solution.py:269
  18.6 51.6 %conditional.1 = (bf16[256,1024]{1,0:T(8,128)(2,1)}, f32[1]{0:T(128)}) conditional(s32[]{:T(128)} %bitcast.8, (s32[16,16]{1,0:T(8,128)}, s32[16]{0:T(128)}, s32[18]{0:T(128)S(1)}, bf16[8,64,128]{2,1,0:T(8,128)(2,1)S(1)}, bf16[1024]{0:T(1024)(128)(2,1)}, /*index=5*/bf16[256,1024]{1,0:T(8,128)(2,1)}, ...), branch_computations={%region_0.2_spmd, %region_2.4_spmd, %region_4.6_spmd, %region_6.8_... | conditional | flops 5000000000 | bytes 42010836 | solution.py:331
  18.6 0.0 copy-start.12
  18.6 0.0 copy-start.6
  18.6 0.0 copy-start.18
  18.6 0.0 copy-start.24
  18.6 0.0 copy-start.32
  18.6 0.0 copy-start.40
  18.6 2.6 %branch_3_fun.4 = bf16[16,192,128]{2,1,0:T(8,128)(2,1)} custom-call(s32[16,16]{1,0:T(8,128)} %get-tuple-element.183.mask_ref, s32[16]{0:T(128)} %get-tuple-element.180.len_ref, s32[18]{0:T(128)S(1)} %get-tuple-element.181.meta_ref, bf16[8,64,128]{2,1,0:T(8,128)(2,1)S(1)} %get-tuple-element.184.held_ref), custom_call_target="tpu_custom_call" | custom-call | tf_op jit(solution)/shard_map/cond/branch_3_fun/pallas_call | solution.py:280
  21.2 10.4 %all-to-all-start.6 = ((bf16[16,192,128]{2,1,0:T(8,128)(2,1)}), bf16[16,192,128]{2,1,0:T(8,128)(2,1)S(1)}, u32[]{:S(2)}, u32[]{:S(2)}) async-start(bf16[16,192,128]{2,1,0:T(8,128)(2,1)} %branch_3_fun.4), calls=%async_computation.6 | async-start | bytes 1572864 | tf_op jit(solution)/shard_map/cond/branch_3_fun/all_to_all | solution.py:288
  31.6 0.0 copy-done.12
  31.6 0.0 copy-done.6
  31.7 0.0 copy-done.18
  31.7 0.0 copy-done.24
  31.7 0.0 copy-done.32
  31.7 0.0 copy-done.40
  31.7 4.7 %branch_3_fun.5 = (f32[8,1,256]{2,1,0:T(1,128)S(1)}, f32[8,1,256]{2,1,0:T(1,128)S(1)}, f32[8,128,256]{2,1,0:T(8,128)S(1)}, f32[1,1536]{1,0:T(1,128)S(1)}, f32[15...) custom-call(s32[16,16]{1,0:T(8,128)S(1)} %copy-done.6, ...), custom_call_target="tpu_custom_call" | custom-call | flops 1000000000 | bytes 5000000 | tf_op jit(solution)/shard_map/cond/branch_3_fun/pallas_call | solution.py:291
  36.4 23.2 %all-to-all-done.6.got_ref = bf16[16,192,128]{2,1,0:T(8,128)(2,1)S(1)} async-done(((bf16[16,192,128]{2,1,0:T(8,128)(2,1)}), bf16[16,192,128]{2,1,0:T(8,128)(2,1)S(1)}, u32[]{:S(2)}, u32[]{:S(2)}) %all-to-all-start.6) | async-done | bytes 786464 | tf_op jit(solution)/shard_map/cond/branch_3_fun/all_to_all | solution.py:288
  59.6 1.1 %branch_3_fun.7 = f32[8,1,128]{2,1,0:T(1,128)} custom-call(bf16[16,192,128]{2,1,0:T(8,128)(2,1)S(1)} %all-to-all-done.6.got_ref, f32[1,1536]{1,0:T(1,128)S(1)} %get-tuple-element.192.across_ref, f32[8,128]{1,0:T(8,128)S(1)} %get-tuple-element.193.lastq_ref, f32[8,128]{1,0:T(8,128)S(1)} %get-tuple-element.194.probes_ref, ...), custom_call_target="tpu_custom_call" | custom-call | tf_op jit(solution)/shard_map/cond/branch_3_fun/pallas_call | solution.py:304
  60.7 3.3 %all-to-all-start.7 = ((f32[8,1,128]{2,1,0:T(1,128)}), f32[8,1,128]{2,1,0:T(1,128)S(1)}, u32[]{:S(2)}, u32[]{:S(2)}) async-start(f32[8,1,128]{2,1,0:T(1,128)} %branch_3_fun.7), calls=%async_computation.7 | async-start | bytes 8192 | tf_op jit(solution)/shard_map/cond/branch_3_fun/all_to_all | solution.py:311
  64.0 1.3 %branch_3_fun.6 = bf16[256,1024]{1,0:T(8,128)(2,1)} custom-call(s32[16]{0:T(128)S(1)} %copy-done.32, s32[18]{0:T(128)S(1)} %get-tuple-element.181.meta_ref, bf16[256,1024]{1,0:T(8,128)(2,1)S(1)} %copy-done.40, bf16[16,192,128]{2,1,0:T(8,128)(2,1)S(1)} %all-to-all-done.6.got_ref, f32[1536,128]{1,0:T(8,128)S(1)} %get-tuple-element.188.down_ref, ...), custom_call_target="tpu_custom_call" | custom-call | flops 4000000000 | bytes 5000000 | tf_op jit(solution)/shard_map/cond/branch_3_fun/pallas_call | solution.py:312
  65.3 4.2 %all-to-all-done.7 = f32[8,1,128]{2,1,0:T(1,128)S(1)} async-done(((f32[8,1,128]{2,1,0:T(1,128)}), f32[8,1,128]{2,1,0:T(1,128)S(1)}, u32[]{:S(2)}, u32[]{:S(2)}) %all-to-all-start.7) | async-done | bytes 4128 | tf_op jit(solution)/shard_map/cond/branch_3_fun/all_to_all | solution.py:311
  69.5 0.6 slice_reduce_fusion.3
  (1 shorter events, 0.0 us)
Async XLA Ops:
  2.4 16.2 %all-to-all-start.16 = ((bf16[8,64,128]{2,1,0:T(8,128)(2,1)}), bf16[8,64,128]{2,1,0:T(8,128)(2,1)S(1)}, u32[]{:S(2)}, u32[]{:S(2)}) async-start(bf16[8,64,128]{2,1,0:T(8,128)(2,1)} %shard_map.110), calls=%async_computation.16 | async-start | bytes 262144 | tf_op jit(solution)/shard_map/all_to_all | solution.py:269
  18.6 13.1 %copy-start.12 = (bf16[1024]{0:T(1024)(128)(2,1)S(1)}, bf16[1024]{0:T(1024)(128)(2,1)}, u32[]{:S(2)}) copy-start(bf16[1024]{0:T(1024)(128)(2,1)} %get-tuple-element.292) | copy-start | bytes 6148 | tf_op jit(solution)/shard_map/cond
  18.6 13.1 %copy-start.6 = (s32[16,16]{1,0:T(8,128)S(1)}, s32[16,16]{1,0:T(8,128)}, u32[]{:S(2)}) copy-start(s32[16,16]{1,0:T(8,128)} %get-tuple-element.183.mask_ref) | copy-start | bytes 3076 | tf_op jit(solution)/shard_map/cond
  18.6 13.1 %copy-start.18 = (bf16[256,128]{1,0:T(8,128)(2,1)S(1)}, bf16[256,128]{1,0:T(8,128)(2,1)}, u32[]{:S(2)}) copy-start(bf16[256,128]{1,0:T(8,128)(2,1)} %get-tuple-element.185.k_ref) | copy-start | bytes 196612 | tf_op jit(solution)/shard_map/cond
  18.6 13.1 %copy-start.24 = (bf16[256,128]{1,0:T(8,128)(2,1)S(1)}, bf16[256,128]{1,0:T(8,128)(2,1)}, u32[]{:S(2)}) copy-start(bf16[256,128]{1,0:T(8,128)(2,1)} %get-tuple-element.186.v_ref) | copy-start | bytes 196612 | tf_op jit(solution)/shard_map/cond
  18.6 13.1 %copy-start.32 = (s32[16]{0:T(128)S(1)}, s32[16]{0:T(128)}, u32[]{:S(2)}) copy-start(s32[16]{0:T(128)} %get-tuple-element.180.len_ref) | copy-start | bytes 196 | tf_op jit(solution)/shard_map/cond
  18.6 13.1 %copy-start.40 = (bf16[256,1024]{1,0:T(8,128)(2,1)S(1)}, bf16[256,1024]{1,0:T(8,128)(2,1)}, u32[]{:S(2)}) copy-start(bf16[256,1024]{1,0:T(8,128)(2,1)} %get-tuple-element.300.q_ref) | copy-start | bytes 1572868 | tf_op jit(solution)/shard_map/cond
  21.2 38.4 %all-to-all-start.6 = ((bf16[16,192,128]{2,1,0:T(8,128)(2,1)}), bf16[16,192,128]{2,1,0:T(8,128)(2,1)S(1)}, u32[]{:S(2)}, u32[]{:S(2)}) async-start(bf16[16,192,128]{2,1,0:T(8,128)(2,1)} %branch_3_fun.4), calls=%async_computation.6 | async-start | bytes 1572864 | tf_op jit(solution)/shard_map/cond/branch_3_fun/all_to_all | solution.py:288
  60.7 8.8 %all-to-all-start.7 = ((f32[8,1,128]{2,1,0:T(1,128)}), f32[8,1,128]{2,1,0:T(1,128)S(1)}, u32[]{:S(2)}, u32[]{:S(2)}) async-start(f32[8,1,128]{2,1,0:T(1,128)} %branch_3_fun.7), calls=%async_computation.7 | async-start | bytes 8192 | tf_op jit(solution)/shard_map/cond/branch_3_fun/all_to_all | solution.py:311
